TPU v7x, 128 devices: a whole 4x4x4 slice. The times are simulated.
128 devices in a mesh: dp: 16 (over x_hi, z, core), tensor: 8 (over y, x_lo).
Axes of the slice: x: 4 (x_hi: 2, x_lo: 2; x = x_hi * 2 + x_lo), y: 4, z: 4, core: 2. Of those that a mesh axis runs over, the one named last changes fastest.
Arguments:
- hidden_in: bfloat16 [32, 96, 8192], P('dp', 'tensor'), may hold values from -40 to 40
- norm_gain: float32 [8192], replicated, may hold values from 0.5 to 1.5
- w_query: bfloat16 [8192, 4096], P(None, 'tensor'), may hold values from -1.41421356 to 1.41421356
- w_key: bfloat16 [8192, 1024], P(None, 'tensor'), may hold values from -0.044194174 to 0.044194174
- w_value: bfloat16 [8192, 1024], P(None, 'tensor'), may hold values from -0.0625 to 0.0625
- w_out: bfloat16 [4096, 8192], P('tensor'), may hold values from -0.09375 to 0.09375
- cotangent: bfloat16 [32, 96, 8192], P('dp', 'tensor'), may hold values from -6 to 6
Outputs:
- layer_out: bfloat16 [32, 96, 8192], P('dp', 'tensor')
- input_grad: bfloat16 [32, 96, 8192], P('dp', 'tensor')
- query_grad: float32 [8192, 4096], P('dp', 'tensor')
- key_grad: float32 [8192, 1024], P('dp', 'tensor')
- value_grad: float32 [8192, 1024], P('dp', 'tensor')
- out_grad: float32 [4096, 8192], P('tensor', 'dp')
- gain_grad: float32 [8192], P(('dp', 'tensor'))
All inputs are finite; a program needn't handle non-finite values.
Results may differ from a plain program's by a relative error of at most 0.035.
Values may be sent and summed in bfloat16 or wider, within the bound.
A program may use at most 256 MiB of HBM per device.

v0:
```python
import jax
import jax.numpy as jnp
from jax import lax
from jax.sharding import PartitionSpec as P

HD = 128


EPS = 1e-05
ROPE_BASE = 10000.0


def rope_tables(length, head_width):
    half_width = head_width // 2
    frequency = ROPE_BASE ** (-2.0 * jnp.arange(half_width, dtype=jnp.float32) / head_width)
    angles = jnp.arange(length, dtype=jnp.float32)[:, None] * frequency[None, :]
    cosine_table = jnp.concatenate([jnp.cos(angles), jnp.cos(angles)], axis=1)
    sine_table = jnp.concatenate([jnp.sin(angles), jnp.sin(angles)], axis=1)
    return (cosine_table, sine_table)


def rotate(vectors, cosine_table, sine_table):
    half_width = vectors.shape[-1] // 2
    turned = jnp.concatenate([-vectors[..., half_width:], vectors[..., :half_width]], axis=-1)
    return vectors * cosine_table[:, None, :] + turned * sine_table[:, None, :]


def unrotate(gradient, cosine_table, sine_table):
    half_width = gradient.shape[-1] // 2
    scaled = gradient * sine_table[:, None, :]
    rotated_back = jnp.concatenate([scaled[..., half_width:], -scaled[..., :half_width]], axis=-1)
    return gradient * cosine_table[:, None, :] + rotated_back


def normalize(row_block, norm_gain):
    as_float = row_block.astype(jnp.float32)
    inverse = lax.rsqrt(jnp.mean(as_float * as_float, axis=-1, keepdims=True) + EPS)
    return (as_float * inverse * norm_gain).astype(jnp.bfloat16)


def attention_weights(query_rot, key_rot):
    seq_count, length, head_count, head_width = query_rot.shape
    key_heads = key_rot.shape[2]
    grouped = query_rot.reshape(seq_count, length, key_heads, head_count // key_heads, head_width)
    logits = jnp.einsum(
        "bqgjd,bkgd->bgjqk", grouped, key_rot, preferred_element_type=jnp.float32
    ) * head_width ** (-0.5)
    rows_at = lax.broadcasted_iota(jnp.int32, (length, length), 0)
    cols_at = lax.broadcasted_iota(jnp.int32, (length, length), 1)
    logits = jnp.where(rows_at >= cols_at, logits, -1e30)
    largest = jnp.max(logits, axis=-1, keepdims=True)
    powers = jnp.exp(logits - largest)
    return powers / jnp.sum(powers, axis=-1, keepdims=True)


def attention_mix(attn_probs, values):
    weights = attn_probs.astype(jnp.bfloat16)
    seq_count, key_heads, per_group, length, _ = weights.shape
    mixed_heads = jnp.einsum(
        "bgjqk,bkgd->bqgjd", weights, values, preferred_element_type=jnp.float32
    )
    return mixed_heads.reshape(seq_count, length, key_heads * per_group * values.shape[-1]).astype(
        jnp.bfloat16
    )


def attention_grads(query_rot, key_rot, values, grad_mixed):
    seq_count, length, head_count, head_width = query_rot.shape
    key_heads = key_rot.shape[2]
    per_group = head_count // key_heads
    attn_probs = attention_weights(query_rot, key_rot)
    weights = attn_probs.astype(jnp.bfloat16)
    grouped_grad = grad_mixed.reshape(seq_count, length, key_heads, per_group, head_width)
    grouped_query = query_rot.reshape(seq_count, length, key_heads, per_group, head_width)
    dvalues = jnp.einsum(
        "bgjqk,bqgjd->bkgd", weights, grouped_grad, preferred_element_type=jnp.float32
    )
    prob_grad = jnp.einsum(
        "bqgjd,bkgd->bgjqk", grouped_grad, values, preferred_element_type=jnp.float32
    )
    row_delta = jnp.sum(attn_probs * prob_grad, axis=-1, keepdims=True)
    score_grad = (attn_probs * (prob_grad - row_delta) * head_width ** (-0.5)).astype(jnp.bfloat16)
    dquery_rot = jnp.einsum(
        "bgjqk,bkgd->bqgjd", score_grad, key_rot, preferred_element_type=jnp.float32
    )
    dkey_rot = jnp.einsum(
        "bgjqk,bqgjd->bkgd", score_grad, grouped_query, preferred_element_type=jnp.float32
    )
    return (dquery_rot.reshape(seq_count, length, head_count, head_width), dkey_rot, dvalues)


def shards(hidden_in, norm_gain, w_query, w_key, w_value, w_out, cotangent):
    seq_count, own_len, model_width = hidden_in.shape
    tensor_size = lax.axis_size("tensor")
    tensor_at = lax.axis_index("tensor")
    length = own_len * tensor_size
    query_cols = w_query.shape[1]
    key_cols = w_key.shape[1]
    head_count = query_cols // HD
    key_heads = key_cols // HD
    w_joint = jnp.concatenate([w_query, w_key, w_value], axis=1)
    joint_cols = w_joint.shape[1]
    cosine_table, sine_table = rope_tables(length, HD)
    spans = [(0, seq_count)]
    start_at, stop_at = spans[0]
    block_len = stop_at - start_at
    whole_rows = lax.all_gather(hidden_in, "tensor", axis=1, tiled=True)
    normed = normalize(whole_rows, norm_gain)
    flat_normed = normed.reshape(block_len * length, model_width)
    joint = jnp.dot(flat_normed, w_joint, preferred_element_type=jnp.float32)
    joint = joint.reshape(block_len, length, head_count + 2 * key_heads, HD)
    query_rot = rotate(joint[:, :, :head_count], cosine_table, sine_table).astype(jnp.bfloat16)
    key_rot = rotate(
        joint[:, :, head_count : head_count + key_heads], cosine_table, sine_table
    ).astype(jnp.bfloat16)
    values = joint[:, :, head_count + key_heads :].astype(jnp.bfloat16)
    mixed_heads = attention_mix(attention_weights(query_rot, key_rot), values)
    partial_value = jnp.dot(
        mixed_heads.reshape(block_len * length, query_cols),
        w_out,
        preferred_element_type=jnp.float32,
    )
    partial_value = partial_value.reshape(block_len, length, model_width)
    summed = lax.psum(partial_value.astype(jnp.bfloat16), "tensor").astype(jnp.float32)
    share = lax.dynamic_slice_in_dim(summed, tensor_at * own_len, own_len, 1)
    outputs = (hidden_in.astype(jnp.float32) + share).astype(jnp.bfloat16)
    saved = [(normed, query_rot, key_rot, values, mixed_heads)]
    proj_total = jnp.zeros((query_cols, model_width), jnp.float32)
    mixed_grads = []
    for (start_at, stop_at), stored in zip(spans, saved):
        block_len = stop_at - start_at
        grad_rows = lax.all_gather(cotangent, "tensor", axis=1, tiled=True)
        flat_grad = grad_rows.reshape(block_len * length, model_width)
        flat_mixed = stored[4].reshape(block_len * length, query_cols)
        proj_total = lax.dot_general(
            flat_mixed, flat_grad, (((0,), (0,)), ((), ())), preferred_element_type=jnp.float32
        )
        grad_mixed = lax.dot_general(
            flat_grad, w_out, (((1,), (1,)), ((), ())), preferred_element_type=jnp.float32
        )
        mixed_grads.append(
            grad_mixed.astype(jnp.bfloat16).reshape(block_len, length, head_count, HD)
        )
    joint_total = jnp.zeros((model_width, joint_cols), jnp.float32)
    gain_total = jnp.zeros((model_width,), jnp.float32)
    input_grads = []
    for (start_at, stop_at), stored, grad_mixed in zip(spans, saved, mixed_grads):
        normed, query_rot, key_rot, values, mixed_heads = stored
        block_len = stop_at - start_at
        dquery_rot, dkey_rot, dvalues = attention_grads(query_rot, key_rot, values, grad_mixed)
        grad_query = unrotate(dquery_rot, cosine_table, sine_table).astype(jnp.bfloat16)
        grad_key = unrotate(dkey_rot, cosine_table, sine_table).astype(jnp.bfloat16)
        grad_value = dvalues.astype(jnp.bfloat16)
        grad_joint = jnp.concatenate(
            [
                grad_query.reshape(block_len * length, query_cols),
                grad_key.reshape(block_len * length, key_cols),
                grad_value.reshape(block_len * length, key_cols),
            ],
            axis=1,
        )
        flat_normed = normed.reshape(block_len * length, model_width)
        joint_total = lax.dot_general(
            flat_normed, grad_joint, (((0,), (0,)), ((), ())), preferred_element_type=jnp.float32
        )
        normed_part = lax.dot_general(
            grad_joint, w_joint, (((1,), (1,)), ((), ())), preferred_element_type=jnp.float32
        )
        normed_part = normed_part.reshape(block_len, length, model_width)
        summed_grad = lax.psum(normed_part.astype(jnp.bfloat16), "tensor").astype(jnp.float32)
        normed_grad = lax.dynamic_slice_in_dim(summed_grad, tensor_at * own_len, own_len, 1)
        as_float = hidden_in.astype(jnp.float32)
        inverse = lax.rsqrt(jnp.mean(as_float * as_float, axis=-1, keepdims=True) + EPS)
        scaled_in = as_float * inverse
        weighted = normed_grad * norm_gain
        input_grad = cotangent.astype(jnp.float32) + inverse * (
            weighted - scaled_in * jnp.mean(weighted * scaled_in, axis=-1, keepdims=True)
        )
        input_grads.append(input_grad.astype(jnp.bfloat16))
        gain_total = jnp.sum(normed_grad * scaled_in, axis=(0, 1))
    joint_share, proj_share = (
        lax.psum_scatter(
            joint_total.astype(jnp.bfloat16), "dp", scatter_dimension=0, tiled=True
        ).astype(jnp.float32),
        lax.psum_scatter(
            proj_total.astype(jnp.bfloat16), "dp", scatter_dimension=1, tiled=True
        ).astype(jnp.float32),
    )
    gain_share = lax.psum_scatter(gain_total, ("dp", "tensor"), scatter_dimension=0, tiled=True)
    query_share = joint_share[:, :query_cols]
    key_share = joint_share[:, query_cols : query_cols + key_cols]
    value_share = joint_share[:, query_cols + key_cols :]
    return (outputs, input_grads[0], query_share, key_share, value_share, proj_share, gain_share)


def solution(mesh):
    return jax.shard_map(
        shards,
        mesh=mesh,
        in_specs=(
            P("dp", "tensor", None),
            P(),
            P(None, "tensor"),
            P(None, "tensor"),
            P(None, "tensor"),
            P("tensor", None),
            P("dp", "tensor", None),
        ),
        out_specs=(
            P("dp", "tensor", None),
            P("dp", "tensor", None),
            P("dp", "tensor"),
            P("dp", "tensor"),
            P("dp", "tensor"),
            P("tensor", "dp"),
            P(("dp", "tensor")),
        ),
        check_vma=False,
    )
```

profile of v0, /device:TPU:1, one launch (start us, length us, event | category | flops | bytes accessed | tf_op | source)
XLA Modules:
  0.0 702.6 jit_solution(18257078442512082710)
XLA Ops:
  7.2 0.7 all-gather.3.cloned.1.call-update
  7.9 0.7 all-gather.5.cloned.1.call-update
  8.8 7.5 %constant_dynamic-update-slice_fusion.2 = bf16[8192,768]{1,0:T(8,128)(2,1)} fusion(bf16[8192,512]{1,0:T(8,128)(2,1)} %param.9), kind=kLoop, calls=%fused_computation.81 | loop fusion | bytes 16777216
  16.3 1.6 constant_dynamic-update-slice_fusion.1
  17.9 1.6 constant_dynamic-update-slice_fusion
  19.5 16.6 %copy.57 = bf16[768,8192]{1,0:T(8,128)(2,1)} copy(bf16[768,8192]{0,1:T(8,128)(2,1)} %bitcast.107) | data formatting | bytes 25165824 | tf_op jit(solution)/shard_map/dot_general | solution.py:110
  36.0 0.2 fusion.39
  36.3 47.7 %all-gather.3.cloned.1.call-done = bf16[2,96,8192]{2,0,1:T(2,128)(2,1)} async-done(((bf16[2,12,8192]{2,0,1:T(2,128)(2,1)}), bf16[2,96,8192]{2,0,1:T(2,128)(2,1)}) %all-gather.3.cloned.1.call-update) | async-done | bytes 3145744 | tf_op jit(solution)/shard_map/all_gather | solution.py:107
  84.1 5.2 fusion.1
  89.3 4.7 fusion.3
  94.0 7.5 %fusion.4 = f32[2,96,6,128]{3,1,2,0:T(8,128)S(1)} fusion(bf16[6,128,8192,1]{2,1,0,3:T(8,128)(2,1)} %bitcast.109, bf16[2,96,8192]{2,1,0:T(8,128)(2,1)S(1)} %fusion.3), kind=kOutput, calls=%fused_computation.10 | convolution fusion | flops 2415919104 | bytes 16318464 | tf_op jit(solution)/shard_map/dot_general | solution.py:110
  102.1 0.7 copy-done.4
  102.8 0.3 fusion.50
  103.2 0.9 fusion.12
  104.1 52.7 %all-gather.5.cloned.1.call-done = bf16[2,96,8192]{2,0,1:T(2,128)(2,1)} async-done(((bf16[2,12,8192]{2,0,1:T(2,128)(2,1)}), bf16[2,96,8192]{2,0,1:T(2,128)(2,1)}) %all-gather.5.cloned.1.call-update) | async-done | bytes 3145744 | tf_op jit(solution)/shard_map/all_gather | solution.py:132
  156.8 3.7 copy.61
  160.4 7.0 convolution_convert_fusion.4
  167.4 1.7 reshape.170
  169.1 1.9 fusion.13
  170.9 1.3 multiply_reduce_fusion
  172.3 1.8 broadcast_multiply_fusion
  174.2 1.8 bitcast_multiply_fusion.1
  176.0 0.8 copy.59
  176.8 1.7 convert_element_type.102
  178.5 7.1 %convolution_convert_fusion.2 = bf16[2,96,8192]{2,1,0:T(8,128)(2,1)} fusion(bf16[2,96,512]{2,1,0:T(8,128)(2,1)} %convert_element_type.102, bf16[512,8192]{1,0:T(8,128)(2,1)} %param.12), kind=kOutput, calls=%fused_computation.3 | convolution fusion | flops 1612185600 | bytes 11730944 | tf_op jit(solution)/shard_map/dot_general | solution.py:118
  186.0 0.3 copy.66
  186.3 0.3 copy.64
  186.9 0.4 copy-done.16
  187.3 10.4 %convolution_convert_fusion.1 = bf16[192,8192]{1,0:T(8,128)(2,1)} fusion(bf16[8192,768]{1,0:T(8,128)(2,1)} %constant_dynamic-update-slice_fusion, bf16[192,128]{1,0:T(8,128)(2,1)S(1)} %bitcast.118, bf16[192,128]{1,0:T(8,128)(2,1)S(1)} %bitcast.116, bf16[192,512]{1,0:T(8,128)(2,1)S(1)} %fusion.21), kind=kOutput, calls=%fused_computation.2 | convolution fusion | flops 2418376704 | bytes 16023552 | tf_op jit(solution)/shard_map/dot_general | solution.py:166
  197.8 0.3 reduce-scatter.5.cloned.1.call-start
  198.0 0.6 copy-done.5
  198.7 9.9 %bitcast_convert_fusion = bf16[512,8192]{1,0:T(8,128)(2,1)} fusion(bf16[2,96,512]{2,1,0:T(8,128)(2,1)S(1)} %copy-done.5, bf16[2,96,8192]{2,0,1:T(2,128)(2,1)} %all-gather.5.cloned.1.call-done), kind=kOutput, calls=%fused_computation | convolution fusion | flops 1614807040 | bytes 11730944 | tf_op jit(solution)/shard_map/dot_general | solution.py:135
  208.6 0.7 copy-done.17
  209.4 6.5 convolution_convert_fusion
  215.9 1.0 copy-done
  216.8 0.5 fusion.20
  217.4 241.8 %all-reduce.4.cloned.1.call-done = (bf16[2,96,8192]{2,1,0:T(8,128)(2,1)}, bf16[2,96,8192]{2,1,0:T(8,128)(2,1)}) async-done(((bf16[2,96,8192]{2,1,0:T(8,128)(2,1)}, bf16[2,96,8192]{2,1,0:T(8,128)(2,1)}), (bf16[2,96,8192]{2,1,0:T(8,128)(2,1)}, bf16[2,96,8192]{2,1,0:T(8,128)(2,1)})) %all-reduce.4.cloned.1.call-update) | async-done | bytes 6291472 | tf_op jit(solution)/shard_map/psum | solution.py:124
  459.1 1.9 fusion.18
  461.1 2.1 fusion.16
  463.2 1.2 copy.69
  464.4 1.2 copy.70
  465.5 73.4 %all-reduce = f32[8192]{0:T(1024)S(1)} all-reduce(f32[8192]{0:T(1024)S(1)} %get-tuple-element.35), channel_id=4, replica_groups=mesh['dp'=16,'tensor'=8] {'dp','tensor'}, use_global_device_ids=true, to_apply=%region_11.12.clone | all-reduce | flops 8192 | bytes 65536
  538.9 0.6 dynamic-slice
  539.5 27.1 %reduce-scatter.5.cloned.1.call-done = bf16[512,512]{1,0:T(8,128)(2,1)} async-done(((bf16[512,8192]{1,0:T(8,128)(2,1)}), bf16[512,512]{1,0:T(8,128)(2,1)}) %reduce-scatter.5.cloned.1.call-update) | async-done | bytes 524304 | tf_op jit(solution)/shard_map/reduce_scatter | solution.py:185
  566.5 2.1 convert_element_type.121
  568.7 123.4 %reduce-scatter.3.cloned.1.call-done = bf16[512,768]{1,0:T(8,128)(2,1)} async-done(((bf16[8192,768]{1,0:T(8,128)(2,1)}), bf16[512,768]{1,0:T(8,128)(2,1)}) %reduce-scatter.3.cloned.1.call-update) | async-done | bytes 786448 | tf_op jit(solution)/shard_map/reduce_scatter | solution.py:182
  692.1 2.1 slice.72
  694.3 1.8 fusion.47
  (62 shorter events, 1.9 us)
Async XLA Ops:
  7.2 76.9 %all-gather.3.cloned.1.call-start = ((), (), s32[]{:S(2)}) async-start(), calls=%async_computation.2 | async-start | bytes 3538944 | tf_op jit(solution)/shard_map/all_gather | solution.py:107
  7.9 148.9 %all-gather.5.cloned.1.call-start = ((), (), s32[]{:S(2)}) async-start(), calls=%async_computation.3 | async-start | bytes 3538944 | tf_op jit(solution)/shard_map/all_gather | solution.py:132
  8.6 450.5 %all-reduce.4.cloned.1.call-start = ((), (), s32[]{:S(2)}) async-start(), calls=%async_computation.6 | async-start | bytes 12582912 | tf_op jit(solution)/shard_map/psum | solution.py:124
  8.7 7.5 %copy-start.2 = (bf16[8192,128]{1,0:T(8,128)(2,1)S(1)}, bf16[8192,128]{1,0:T(8,128)(2,1)}, u32[]{:S(2)}) copy-start(bf16[8192,128]{1,0:T(8,128)(2,1)} %param.10) | copy-start | bytes 6291460
  8.7 9.1 %copy-start.3 = (bf16[8192,128]{1,0:T(8,128)(2,1)S(1)}, bf16[8192,128]{1,0:T(8,128)(2,1)}, u32[]{:S(2)}) copy-start(bf16[8192,128]{1,0:T(8,128)(2,1)} %param.11) | copy-start | bytes 6291460
  19.5 69.9 %copy-start.14 = (f32[8192]{0:T(1024)S(1)}, f32[8192]{0:T(1024)}, u32[]{:S(2)}) copy-start(f32[8192]{0:T(1024)} %param.8) | copy-start | bytes 98308
  36.3 65.6 %copy-start.8 = (f32[96,128]{1,0:T(8,128)}, f32[96,128]{1,0:T(8,128)S(1)}, u32[]{:S(2)}) copy-start(f32[96,128]{1,0:T(8,128)S(1)} %get-tuple-element.62) | copy-start | bytes 147460
  36.3 65.6 %copy-start.9 = (f32[96,128]{1,0:T(8,128)}, f32[96,128]{1,0:T(8,128)S(1)}, u32[]{:S(2)}) copy-start(f32[96,128]{1,0:T(8,128)S(1)} %get-tuple-element.61) | copy-start | bytes 147460
  101.5 1.7 copy-start.1
  101.7 1.4 copy-start.12
  102.1 0.7 copy-start.4
  169.1 6.9 copy-start.18
  178.5 7.1 %copy-start.11 = (f32[2,96,1,128]{3,1,2,0:T(8,128)S(1)}, f32[2,96,1,128]{3,1,2,0:T(8,128)}, u32[]{:S(2)}) copy-start(f32[2,96,1,128]{3,1,2,0:T(8,128)} %get-tuple-element.57) | copy-start | bytes 294916
  178.5 7.8 %copy-start.6 = (f32[2,128,4,96]{1,3,2,0:T(8,128)S(1)}, f32[2,128,4,96]{1,3,2,0:T(8,128)}, u32[]{:S(2)}) copy-start(f32[2,128,4,96]{1,3,2,0:T(8,128)} %get-tuple-element.60) | copy-start | bytes 1179652
  178.5 8.1 %copy-start.10 = (f32[96,128]{1,0:T(8,128)S(1)}, f32[96,128]{1,0:T(8,128)}, u32[]{:S(2)}) copy-start(f32[96,128]{1,0:T(8,128)} %copy-done.9) | copy-start | bytes 147460
  178.5 8.1 %copy-start.13 = (f32[2,96,1,128]{3,1,2,0:T(8,128)S(1)}, f32[2,96,1,128]{3,1,2,0:T(8,128)}, u32[]{:S(2)}) copy-start(f32[2,96,1,128]{3,1,2,0:T(8,128)} %get-tuple-element.58) | copy-start | bytes 294916
  185.6 1.7 copy-start.19
  186.7 0.6 copy-start.16
  197.7 0.9 copy-start.5
  197.8 368.8 %reduce-scatter.5.cloned.1.call-start = ((), (), s32[]{:S(2)}) async-start(), calls=%async_computation.5 | async-start | bytes 8912896 | tf_op jit(solution)/shard_map/reduce_scatter | solution.py:185
  208.5 0.8 copy-start.17
  208.6 0.8 copy-start.20
  208.6 483.6 %reduce-scatter.3.cloned.1.call-start = ((), (), s32[]{:S(2)}) async-start(), calls=%async_computation.4 | async-start | bytes 13369344 | tf_op jit(solution)/shard_map/reduce_scatter | solution.py:182
  215.8 1.0 copy-start
  215.8 243.3 %copy-start.15 = (f32[8192]{0:T(1024)S(1)}, f32[8192]{0:T(1024)}, u32[]{:S(2)}) copy-start(f32[8192]{0:T(1024)} %param.8) | copy-start | bytes 98308
  215.8 245.2 %copy-start.7 = (bf16[2,12,8192]{2,0,1:T(2,128)(2,1)S(1)}, bf16[2,12,8192]{2,0,1:T(2,128)(2,1)}, u32[]{:S(2)}) copy-start(bf16[2,12,8192]{2,0,1:T(2,128)(2,1)} %param.13) | copy-start | bytes 1179652
Sparse Core Ops, SparseCore 0:
  9.6 74.3 all-gather.2
  85.7 71.0 all-gather.4
  197.9 261.1 all-reduce.3
  463.3 103.2 reduce-scatter.4
  570.7 121.3 reduce-scatter.2
where the time goes:
time: 704 us; the launch traced here: 703 us
  waiting for transfers between devices  494 us (70%)
  blocking collectives  73.4 us (10%)
  matrix products  56.4 us (8%)
  local copies, waits for them, and re-layouts  45.9 us (7%)
  other arithmetic  18.4 us (3%)
  between operations  14.1 us (2%)
    psum x1, waiting for transfers between devices, shards(): lax.psum(partial_value.astype(jnp.bfloat16), 'tensor').astype(jnp.float32)  242 us
    reduce_scatter x1, waiting for transfers between devices, shards(): lax.psum_scatter(joint_total.astype(jnp.bfloat16), 'dp', scatter_dimensio...  123 us
    unnamed x1, blocking collectives  73.4 us
    all_gather x1, waiting for transfers between devices, shards(): grad_rows = lax.all_gather(cotangent, 'tensor', axis=1, tiled=True)  52.7 us
    all_gather x1, waiting for transfers between devices, shards(): whole_rows = lax.all_gather(hidden_in, 'tensor', axis=1, tiled=True)  47.7 us
    reduce_scatter x1, waiting for transfers between devices, shards(): lax.psum_scatter(proj_total.astype(jnp.bfloat16), 'dp', scatter_dimension...  27.1 us
    dot_general x1, local copies, waits for them, and re-layouts, shards(): joint = jnp.dot(flat_normed, w_joint, preferred_element_type=jnp.float32)  16.6 us
    unnamed x47, local copies, waits for them, and re-layouts  15.5 us
  transfers between devices with their start and end apart: 5, of which 5 were waited for; matrix products, arithmetic and copies ran while one was open for 10% of the time, Pallas kernels for 0%

commit v1 on v0

v1 whole, which is shorter than its diff:
```python
import jax
import jax.numpy as jnp
import numpy as np
from jax import lax
from jax.experimental import pallas as pl
from jax.experimental.pallas import tpu as pltpu
from jax.sharding import PartitionSpec as P

HD = 128
EPS = 1e-05
ROPE_BASE = 10000.0
BF, F32 = jnp.bfloat16, jnp.float32
SLOTS, ROWS, D = 8, 24, 8192
PAIR, HALF = 2 * ROWS, D // 2
TOK = SLOTS * ROWS
SEQ_ROWS = 12
HEADS = 4
QC, KC = 512, 128
PIECES, PIECE, SLICE = 5, 256, 512
SCALE = HD ** (-0.5)
MESH_ID = pl.DeviceIdType.MESH
MIB = 1024 * 1024


def place():
    dp, tensor = lax.axis_index("dp"), lax.axis_index("tensor")
    core, chip = lax.rem(dp, 2), dp // 2
    z, xh = lax.rem(chip, 4), chip // 4
    y, xl = tensor // 2, lax.rem(tensor, 2)
    here = dict(z=z, xh=xh, core=core, y=y, xl=xl, dp=dp, tensor=tensor)

    def along_z(at):
        return ((xh * 4 + at) * 2 + core, tensor)

    def along_y(at):
        return (dp, at * 2 + xl)

    here["z_up"] = along_z(lax.rem(z + 1, 4))
    here["z_down"] = along_z(lax.rem(z + 3, 4))
    here["y_up"] = along_y(lax.rem(y + 1, 4))
    here["y_down"] = along_y(lax.rem(y + 3, 4))
    here["x_lo"] = (dp, y * 2 + 1 - xl)
    here["x_hi"] = (((1 - xh) * 4 + z) * 2 + core, tensor)
    here["sibling"] = (chip * 2 + 1 - core, tensor)
    here["z_even"] = along_z(z + 1 - 2 * lax.rem(z, 2))
    here["z_odd"] = along_z(3 - z)
    here["y_even"] = along_y(y + 1 - 2 * lax.rem(y, 2))
    here["y_odd"] = along_y(3 - y)
    return here


def greet(devices):
    barrier = pltpu.get_barrier_semaphore()
    for device in devices:
        pl.semaphore_signal(barrier, inc=1, device_id=device, device_id_type=MESH_ID)
    pl.semaphore_wait(barrier, len(devices))


def remote(src, dst, send, recv, device):
    return pltpu.make_async_remote_copy(
        src_ref=src, dst_ref=dst, send_sem=send, recv_sem=recv, device_id=device, device_id_type=MESH_ID
    )


def dot(a, b, ca=1, cb=0):
    return lax.dot_general(a, b, (((ca,), (cb,)), ((), ())), preferred_element_type=F32)


def cols(at, width=SLICE):
    return pl.ds(pl.multiple_of(at * width, width), width)


def layer_kernel(
    hidden, cot, gain, w_query, w_key, w_value, w_out, cosine, sine, bias,
    layer_out, input_grad, query_share, key_share, value_share, out_share, gain_out,
    wq, wkv, wo, rows_n, rows_c, flat_n, flat_c, sib_n, sib_c, turned, turned_sib,
    t_far_r, t_side_r, t_near_r, t_pair_r, far_r, side_r, near_r, pair_r,
    gain_s, gain_r, query_acc, kv_acc, query_rot, key_rot, values, mixed, grad_mixed, grad_query, grad_kv, probs,
    inverse, summed,
    w_sems, wo_sems, a_send, a_recv, s_send, s_recv, d_send, d_recv, t_send, t_recv, g_send, g_recv,
):
    here = place()
    y, xl, z, xh, core = here["y"], here["xl"], here["z"], here["xh"], here["core"]
    y_up, y_down, y_far = lax.rem(y + 1, 4), lax.rem(y + 3, 4), lax.rem(y + 2, 4)
    z_up, z_down, z_far = lax.rem(z + 1, 4), lax.rem(z + 3, 4), lax.rem(z + 2, 4)
    own, mate = here["tensor"], y * 2 + 1 - xl
    toward = ((here["y_up"], y_up), (here["y_down"], y_down))
    toward_z = ((here["z_up"], z_up), (here["z_down"], z_down))
    rows = (rows_n, rows_c)

    loads = (
        pltpu.make_async_copy(w_query, wq, w_sems.at[0]),
        pltpu.make_async_copy(w_key, wkv.at[:, pl.ds(0, KC)], w_sems.at[1]),
        pltpu.make_async_copy(w_value, wkv.at[:, pl.ds(KC, KC)], w_sems.at[2]),
    )

    def load_out(b):
        half, block = b // 16, lax.rem(b, 16)
        return pltpu.make_async_copy(w_out.at[cols(half, PIECE), cols(block)], wo.at[b], wo_sems.at[b])

    for copy in loads:
        copy.start()

    @pl.loop(0, 32)
    def _(b):
        load_out(b).start()

    def square(i, total):
        block = hidden[:, cols(i)].astype(F32)
        return total + jnp.sum(block * block, axis=1, keepdims=True)

    mean = lax.fori_loop(0, 16, square, jnp.zeros((ROWS, 1), F32)) / D
    inverse[...] = jnp.broadcast_to(lax.rsqrt(mean + EPS), (ROWS, 128))

    @pl.loop(0, 8)
    def _(k):
        scale = inverse[:, :1]
        normed = [
            hidden[:, cols(2 * k + p)].astype(F32) * scale * gain[:, cols(2 * k + p)] for p in range(2)
        ]
        rows_n[own, :, cols(k)] = jnp.concatenate(normed, axis=0).astype(BF)
        rows_c[own, :, cols(k)] = jnp.concatenate(
            [cot[:, cols(2 * k + p)].astype(F32) for p in range(2)], axis=0
        ).astype(BF)

    greet([here[name] for name in ("y_up", "y_down", "x_lo", "z_up", "z_down", "x_hi", "sibling")])

    pushed = ([], [])

    def push(a, number, slot, device):
        copy = remote(rows[a].at[slot], rows[a].at[slot], a_send.at[a, number], a_recv.at[a, slot], device)
        copy.start()
        pushed[a].append(copy)

    def landed(a, slot):
        remote(rows[a].at[slot], rows[a].at[slot], a_send.at[a, 0], a_recv.at[a, slot], here["x_lo"]).wait_recv()

    def push_own(a):
        push(a, 0, own, here["x_lo"])
        push(a, 1, own, here["y_up"])
        push(a, 2, own, here["y_down"])

    def push_mate(a):
        landed(a, mate)
        push(a, 3, mate, here["y_up"])
        push(a, 4, mate, here["y_down"])

    def push_far(a):
        landed(a, y_down * 2)
        push(a, 5, y_down * 2, here["y_up"])
        landed(a, y_up * 2 + 1)
        push(a, 6, y_up * 2 + 1, here["y_down"])

    def rest(a):
        landed(a, y_down * 2 + 1)
        landed(a, y_up * 2)
        landed(a, y_far * 2)
        landed(a, y_far * 2 + 1)

    def flatten(a, k):
        chunks = [rows[a][slot, :, cols(k)].astype(F32) for slot in range(SLOTS)]
        return [
            jnp.concatenate([c[p * ROWS : (p + 1) * ROWS] for c in chunks], axis=0).astype(BF) for p in range(2)
        ]

    def to_sibling(number, src, dst):
        return remote(src, dst, s_send.at[number], s_recv.at[number], here["sibling"])

    push_own(0)
    push_mate(0)
    push_far(0)
    push_own(1)
    rest(0)

    query_acc[...] = jnp.zeros_like(query_acc)
    kv_acc[...] = jnp.zeros_like(kv_acc)
    for copy in loads:
        copy.wait()

    @pl.loop(0, 8)
    def _(k):
        for p, block in enumerate(flatten(0, k)):
            flat_n[p, :, cols(k)] = block
            query_acc[...] += dot(block, wq[cols(2 * k + p), :])
            kv_acc[...] += dot(block, wkv[cols(2 * k + p), :])

    share_n = to_sibling(0, flat_n.at[1 - core], sib_n)
    share_n.start()
    push_mate(1)

    def rotated(u):
        return u * cosine[...] + pltpu.roll(u, HD // 2, 1) * sine[...]

    def unrotated(g):
        return g * cosine[...] - pltpu.roll(g, HD // 2, 1) * sine[...]

    def head(h):
        return slice(h * HD, (h + 1) * HD)

    key_rot[...] = rotated(kv_acc[:, :HD]).astype(BF)
    values[...] = kv_acc[:, HD:].astype(BF)
    for h in range(HEADS):
        query_rot[:, head(h)] = rotated(query_acc[:, head(h)]).astype(BF)
    for h in range(HEADS):
        logits = dot(query_rot[:, head(h)], key_rot[...], 1, 1) * SCALE + bias[...]
        powers = jnp.exp(logits - jnp.max(logits, axis=1, keepdims=True))
        prob = powers / jnp.sum(powers, axis=1, keepdims=True)
        probs[h] = prob
        mixed[:, head(h)] = dot(prob.astype(BF), values[...]).astype(BF)
    push_far(1)
    for p in range(2):
        turned[p] = mixed[:, p * PIECE : (p + 1) * PIECE].astype(F32).T.astype(BF)
    share_mixed = to_sibling(1, turned.at[pl.ds(0, 2)], turned_sib.at[pl.ds(0, 2)])
    share_mixed.start()

    @pl.loop(0, 32)
    def _(b):
        load_out(b).wait()

    for copy in pushed[0]:
        copy.wait_send()

    def to_chunks(a, k, blocks):
        for slot in range(SLOTS):
            rows[a][slot, :, cols(k)] = jnp.concatenate(
                [b[slot * ROWS : (slot + 1) * ROWS] for b in blocks], axis=0
            ).astype(BF)

    @pl.loop(0, 8)
    def _(k):
        to_chunks(0, k, [
            dot(mixed[:, :PIECE], wo[2 * k + p]) + dot(mixed[:, PIECE:], wo[16 + 2 * k + p]) for p in range(2)
        ])

    def t_copy(kind, a, way):
        device, at = toward[way]
        slot = (y_far * 2 + way, at * 2 + 1 - way, at * 2 + way)[kind]
        dst = (t_far_r, t_side_r, t_near_r)[kind].at[a, way]
        return remote(rows[a].at[slot], dst, t_send.at[kind, a, way], t_recv.at[kind, a, way], device)

    def t_start(a):
        for kind in range(2):
            for way in range(2):
                t_copy(kind, a, way).start()

    def t_relay(a):
        for way in range(2):
            t_copy(0, a, way).wait()
            slot = toward[way][1] * 2 + way

            @pl.loop(0, 8)
            def _(k, way=way, slot=slot):
                rows[a][slot, :, cols(k)] = (
                    rows[a][slot, :, cols(k)].astype(F32) + t_far_r[a, way, :, cols(k)].astype(F32)
                ).astype(BF)

            t_copy(2, a, way).start()

    def t_total(a, side, k):
        return (
            rows[a][y * 2 + side, :, cols(k)].astype(F32)
            + t_side_r[a, 1 - side, :, cols(k)].astype(F32)
            + t_near_r[a, side, :, cols(k)].astype(F32)
        )

    def t_pair(a):
        return remote(rows[a].at[mate], t_pair_r.at[a], t_send.at[3, a, 0], t_recv.at[3, a, 0], here["x_lo"])

    def t_settle(a):
        for way in range(2):
            t_copy(1, a, way).wait()
            t_copy(2, a, way).wait()

        @pl.loop(0, 8)
        def _(k):
            rows[a][mate, :, cols(k)] = t_total(a, 1 - xl, k).astype(BF)

        t_pair(a).start()

    rest(1)
    t_start(0)

    query_acc[...] = jnp.zeros_like(query_acc)

    @pl.loop(0, 8)
    def _(k):
        for p, block in enumerate(flatten(1, k)):
            flat_c[p, :, cols(k)] = block
            for half in range(2):
                query_acc[:, half * PIECE : (half + 1) * PIECE] += dot(block, wo[half * 16 + 2 * k + p], 1, 1)

    share_c = to_sibling(2, flat_c.at[1 - core], sib_c)
    share_c.start()
    grad_mixed[...] = query_acc[...].astype(BF)

    def product(p, chip, flat, sib):
        total = dot(turned[p], flat[core, :, cols(chip)])
        return total + dot(turned_sib[p], sib[:, cols(chip)])

    def stage(kind, p, way):
        return (kind * 2 + way) * PIECES + p

    def d_copy(kind, p, way):
        device, _ = toward_z[way]
        dst = (far_r, side_r, near_r)[kind].at[way, p]
        return remote(wo.at[stage(kind, p, way)], dst, d_send.at[kind, way, p], d_recv.at[kind, way, p], device)

    def d_pair(p):
        return remote(wo.at[stage(0, p, 0)], pair_r.at[p], d_send.at[3, 0, p], d_recv.at[3, 0, p], here["x_hi"])

    def first_blocks(low, high, flat, sib):
        @pl.loop(low, high)
        def _(p):
            for way in range(2):
                wo[stage(0, p, way)] = product(p, way * 4 + z_far, flat, sib).astype(BF)
                d_copy(0, p, way).start()
            for way in range(2):
                wo[stage(1, p, way)] = product(p, (1 - way) * 4 + toward_z[way][1], flat, sib).astype(BF)
                d_copy(1, p, way).start()

    def second_blocks(low, high, flat, sib):
        @pl.loop(low, high)
        def _(p):
            for way in range(2):
                block = product(p, way * 4 + toward_z[way][1], flat, sib)
                d_copy(0, p, way).wait()
                wo[stage(2, p, way)] = (block + far_r[way, p].astype(F32)).astype(BF)
                d_copy(2, p, way).start()

    def d_total(p, side, flat, sib):
        return (
            product(p, side * 4 + z, flat, sib)
            + side_r[1 - side, p].astype(F32) + near_r[side, p].astype(F32)
        )

    def third_blocks(low, high, flat, sib):
        @pl.loop(low, high)
        def _(p):
            for way in range(2):
                d_copy(1, p, way).wait()
                d_copy(2, p, way).wait()
            wo[stage(0, p, 0)] = d_total(p, 1 - xh, flat, sib).astype(BF)
            d_pair(p).start()

    share_mixed.wait()
    share_c.wait()
    first_blocks(0, 2, flat_c, sib_c)
    t_relay(0)

    dkey = jnp.zeros((TOK, HD), F32)
    dvalues = jnp.zeros((TOK, HD), F32)
    for h in range(HEADS):
        prob = probs[h]
        grad = grad_mixed[:, head(h)]
        dvalues += dot(prob.astype(BF), grad, 0, 0)
        prob_grad = dot(grad, values[...], 1, 1)
        row_delta = jnp.sum(prob * prob_grad, axis=1, keepdims=True)
        score_grad = (prob * (prob_grad - row_delta) * SCALE).astype(BF)
        grad_query[:, head(h)] = unrotated(dot(score_grad, key_rot[...])).astype(BF)
        dkey += dot(score_grad, query_rot[:, head(h)], 0, 0)
    grad_kv[:, :HD] = unrotated(dkey).astype(BF)
    grad_kv[:, HD:] = dvalues.astype(BF)
    for p in range(2):
        turned[2 + p] = grad_query[:, p * PIECE : (p + 1) * PIECE].astype(F32).T.astype(BF)
    turned[4] = grad_kv[...].astype(F32).T.astype(BF)
    share_grads = to_sibling(3, turned.at[pl.ds(2, 3)], turned_sib.at[pl.ds(2, 3)])
    share_grads.start()
    share_n.wait()
    share_grads.wait()
    first_blocks(2, PIECES, flat_n, sib_n)

    for copy in pushed[1]:
        copy.wait_send()

    @pl.loop(0, 8)
    def _(k):
        blocks = []
        for p in range(2):
            at = 2 * k + p
            block = dot(grad_query[...], wq[cols(at), :], 1, 1) + dot(grad_kv[...], wkv[cols(at), :], 1, 1)
            blocks.append(block)
            terms = block.astype(BF).astype(F32) * flat_n[p, :, cols(k)].astype(F32)
            gain_s[0, pl.ds(at, 1), :] = jnp.sum(terms, axis=0, keepdims=True) / gain[:, cols(at)]
        to_chunks(1, k, blocks)

    t_start(1)

    ways = ("sibling", "y_even", "y_odd", "x_lo", "z_even", "z_odd", "x_hi")

    def g_copy(step):
        return remote(gain_s.at[step], gain_r.at[step], g_send.at[step], g_recv.at[step], here[ways[step]])

    def gain_step(step):
        if step:
            g_copy(step - 1).wait()
            gain_s[step] = gain_s[step - 1] + gain_r[step - 1]
        if step < 7:
            g_copy(step).start()

    gain_step(0)
    second_blocks(0, 2, flat_c, sib_c)
    gain_step(1)
    t_settle(0)
    second_blocks(2, PIECES, flat_n, sib_n)
    gain_step(2)
    t_relay(1)
    gain_step(3)
    third_blocks(0, 2, flat_c, sib_c)
    gain_step(4)
    t_settle(1)
    t_pair(0).wait()

    @pl.loop(0, 8)
    def _(k):
        total = t_total(0, xl, k) + t_pair_r[0, :, cols(k)].astype(F32)
        for p in range(2):
            at = cols(2 * k + p)
            layer_out[:, at] = (hidden[:, at].astype(F32) + total[p * ROWS : (p + 1) * ROWS]).astype(BF)

    gain_step(5)
    third_blocks(2, PIECES, flat_n, sib_n)
    gain_step(6)
    t_pair(1).wait()
    scale = inverse[:, :1]

    def weigh(k, total):
        block = t_total(1, xl, k) + t_pair_r[1, :, cols(k)].astype(F32)
        summed[:, cols(k)] = block
        for p in range(2):
            at = cols(2 * k + p)
            scaled = hidden[:, at].astype(F32) * scale
            weighted = block[p * ROWS : (p + 1) * ROWS] * gain[:, at]
            total = total + jnp.sum(weighted * scaled, axis=1, keepdims=True)
        return total

    mean = lax.fori_loop(0, 8, weigh, jnp.zeros((ROWS, 1), F32)) / D

    @pl.loop(0, 8)
    def _(k):
        block = summed[:, cols(k)]
        for p in range(2):
            at = cols(2 * k + p)
            scaled = hidden[:, at].astype(F32) * scale
            weighted = block[p * ROWS : (p + 1) * ROWS] * gain[:, at]
            input_grad[:, at] = (cot[:, at].astype(F32) + scale * (weighted - scaled * mean)).astype(BF)

    gain_step(7)
    gain_out[...] = gain_s[7]

    def final(p, flat, sib):
        total = d_total(p, xh, flat, sib)
        d_pair(p).wait()
        return total + pair_r[p].astype(F32)

    for p in range(2):
        out_share[p * PIECE : (p + 1) * PIECE, :] = final(p, flat_c, sib_c)
    for p in range(2):
        query_share[:, p * PIECE : (p + 1) * PIECE] = final(2 + p, flat_n, sib_n).T
    both = final(4, flat_n, sib_n)
    key_share[...] = both[:KC].T
    value_share[...] = both[KC:].T


def tables(own_len):
    token = np.arange(TOK)
    seq = (token // own_len) % 2
    pos = (token // ROWS) * own_len + token % own_len
    frequency = ROPE_BASE ** (-2.0 * np.arange(HD // 2) / HD)
    angles = pos[:, None] * frequency[None, :]
    cosine = np.concatenate([np.cos(angles), np.cos(angles)], axis=1).astype(np.float32)
    sine = np.concatenate([-np.sin(angles), np.sin(angles)], axis=1).astype(np.float32)
    allowed = (seq[:, None] == seq[None, :]) & (pos[:, None] >= pos[None, :])
    return cosine, sine, np.where(allowed, 0.0, -1e30).astype(np.float32)


def shards(hidden_in, norm_gain, w_query, w_key, w_value, w_out, cotangent):
    dma, vmem = pltpu.SemaphoreType.DMA, pltpu.VMEM
    chunk = (PAIR, HALF)
    block = (PIECE, SLICE)
    at_vmem = pl.BlockSpec(memory_space=pltpu.VMEM)
    at_any = pl.BlockSpec(memory_space=pl.ANY)
    shape = jax.ShapeDtypeStruct
    cosine, sine, bias = tables(SEQ_ROWS)
    layer_out, input_grad, query_share, key_share, value_share, out_share, gain_total = pl.pallas_call(
        layer_kernel,
        out_shape=(
            shape((ROWS, D), BF), shape((ROWS, D), BF), shape((SLICE, QC), F32), shape((SLICE, KC), F32),
            shape((SLICE, KC), F32), shape((QC, SLICE), F32), shape((16, SLICE), F32),
        ),
        in_specs=[at_vmem] * 3 + [at_any] * 4 + [at_vmem] * 3,
        out_specs=tuple([at_vmem] * 7),
        scratch_shapes=[
            vmem((D, QC), BF), vmem((D, 2 * KC), BF), vmem((32,) + block, BF),
            vmem((SLOTS,) + chunk, BF), vmem((SLOTS,) + chunk, BF),
            vmem((2, TOK, HALF), BF), vmem((2, TOK, HALF), BF), vmem((TOK, HALF), BF), vmem((TOK, HALF), BF),
            vmem((PIECES, PIECE, TOK), BF), vmem((PIECES, PIECE, TOK), BF),
            vmem((2, 2) + chunk, BF), vmem((2, 2) + chunk, BF), vmem((2, 2) + chunk, BF), vmem((2,) + chunk, BF),
            vmem((2, PIECES) + block, BF), vmem((2, PIECES) + block, BF), vmem((2, PIECES) + block, BF),
            vmem((PIECES,) + block, BF),
            vmem((8, 16, SLICE), F32), vmem((7, 16, SLICE), F32),
            vmem((TOK, QC), F32), vmem((TOK, 2 * KC), F32),
            vmem((TOK, QC), BF), vmem((TOK, HD), BF), vmem((TOK, HD), BF),
            vmem((TOK, QC), BF), vmem((TOK, QC), BF), vmem((TOK, QC), BF), vmem((TOK, 2 * KC), BF),
            vmem((HEADS, TOK, TOK), F32), vmem((ROWS, 128), F32), vmem(chunk, F32),
            dma((3,)), dma((32,)), dma((2, 7)), dma((2, SLOTS)), dma((4,)), dma((4,)),
            dma((4, 2, PIECES)), dma((4, 2, PIECES)), dma((4, 2, 2)), dma((4, 2, 2)), dma((7,)), dma((7,)),
        ],
        compiler_params=pltpu.CompilerParams(
            collective_id=0, has_side_effects=True, vmem_limit_bytes=61 * MIB
        ),
    )(
        hidden_in.reshape(ROWS, D), cotangent.reshape(ROWS, D), norm_gain.reshape(1, D),
        w_query, w_key, w_value, w_out, jnp.asarray(cosine), jnp.asarray(sine), jnp.asarray(bias),
    )
    share = D // 128
    at = lax.axis_index("dp") * 8 + lax.axis_index("tensor")
    gain_share = lax.dynamic_slice_in_dim(gain_total.reshape(D), at * share, share, 0)
    return (
        layer_out.reshape(hidden_in.shape), input_grad.reshape(hidden_in.shape),
        query_share, key_share, value_share, out_share, gain_share,
    )


def solution(mesh):
    return jax.shard_map(
        shards,
        mesh=mesh,
        in_specs=(
            P("dp", "tensor", None), P(), P(None, "tensor"), P(None, "tensor"), P(None, "tensor"),
            P("tensor", None), P("dp", "tensor", None),
        ),
        out_specs=(
            P("dp", "tensor", None), P("dp", "tensor", None), P("dp", "tensor"), P("dp", "tensor"),
            P("dp", "tensor"), P("tensor", "dp"), P(("dp", "tensor")),
        ),
        check_vma=False,
    )
```

time: 704 us -> 202 us (0.29)
  waiting for transfers between devices: 494 us -> 0 us
  Pallas kernels: 0 us -> 183 us
  blocking collectives: 73.4 us -> 0 us
  matrix products: 56.4 us -> 0 us
  local copies, waits for them, and re-layouts: 45.9 us -> 17.9 us
  other arithmetic: 18.4 us -> 0 us
  between operations: 14.1 us -> 0.67 us
    psum x1 -> x0, waiting for transfers between devices: 242 us -> none  [shards(): lax.psum(partial_value.astype(jnp.bfloat16), 'tensor').astype(jnp.float32)]
    pallas_call x0 -> x1, Pallas kernels: none -> 183 us  [shards(): pl.pallas_call(layer_kernel, out_shape=(shape((ROWS, D), BF), shape((ROWS...]
    reduce_scatter x2 -> x0, waiting for transfers between devices: 151 us -> none  [the longest x1 123 us: shards(): lax.psum_scatter(joint_total.astype(jnp.bfloat16), 'dp', scatter_dimensio...]
    all_gather x2 -> x0, waiting for transfers between devices: 100 us -> none  [the longest x1 52.7 us: shards(): grad_rows = lax.all_gather(cotangent, 'tensor', axis=1, tiled=True)]
    unnamed x1 -> x0, blocking collectives: 73.4 us -> none
    dot_general x12 -> x0, matrix products: 56.4 us -> none  [the longest x1 10.4 us: shards(): lax.dot_general(grad_joint, w_joint, (((1,), (1,)), ((), ())), preferred_...]
    dot_general x1 -> x0, local copies, waits for them, and re-layouts: 16.6 us -> none  [shards(): joint = jnp.dot(flat_normed, w_joint, preferred_element_type=jnp.float32)]
    convert_element_type x6 -> x0, other arithmetic: 9.35 us -> none  [the longest x1 4.66 us: normalize(): return (as_float * inverse * norm_gain).astype(jnp.bfloat16)]
  transfers between devices with their start and end apart: 5 -> 0, of which waited for: 5 -> 0; matrix products, arithmetic and copies ran while one was open for 10% -> 0% of each run, Pallas kernels for 0% -> 0%
where the time goes in v1:
time: 202 us
  Pallas kernels  183 us (91%)
  local copies, waits for them, and re-layouts  17.9 us (9%)
    pallas_call x1, Pallas kernels, shards(): pl.pallas_call(layer_kernel, out_shape=(shape((ROWS, D), BF), shape((ROWS...  183 us
    unnamed x9, local copies, waits for them, and re-layouts  13.4 us

profile of v1, /device:TPU:1, one launch (start us, length us, event | category | flops | bytes accessed | tf_op | source)
XLA Modules:
  0.0 201.7 jit_solution(4005620355656843872)
XLA Ops:
  0.6 1.2 copy.21
  1.9 0.8 reshape.32.hidden
  2.7 1.2 copy.22
  3.9 0.8 reshape.33.cot
  4.8 183.2 %shard_map.153 = (bf16[24,8192]{1,0:T(8,128)(2,1)}, bf16[24,8192]{1,0:T(8,128)(2,1)}, f32[512,512]{1,0:T(8,128)}, f32[512,128]{1,0:T(8,128)}, f32[512,128]{1,0:T...) custom-call(bf16[24,8192]{1,0:T(8,128)(2,1)} %reshape.32.hidden, bf16[24,8192]{1,0:T(8,128)(2,1)} %reshape.33.cot, ...), custom_call_target="tpu_custom_call" | custom-call | tf_op jit(solution)/shard_map/pallas_call | solution.py:484
  188.0 0.8 copy.25
  188.8 0.6 dynamic_slice.3
  189.4 1.1 reshape.35
  190.5 1.2 copy.23
  191.6 1.1 reshape.36
  192.7 1.2 copy.24
  193.9 2.3 %copy.30 = f32[512,512]{1,0:T(8,128)} copy(f32[512,512]{1,0:T(8,128)} %get-tuple-element.44) | data formatting | bytes 2097152
  196.1 1.7 copy.31
  197.8 1.7 copy.32
  199.5 2.3 %copy.33 = f32[512,512]{1,0:T(8,128)} copy(f32[512,512]{1,0:T(8,128)} %get-tuple-element.47) | data formatting | bytes 2097152

commit v2 on v1

v2 whole, which is shorter than its diff:
```python
import jax
import jax.numpy as jnp
import numpy as np
from jax import lax
from jax.experimental import pallas as pl
from jax.experimental.pallas import tpu as pltpu
from jax.sharding import PartitionSpec as P

HD = 128
EPS = 1e-05
ROPE_BASE = 10000.0
BF, F32 = jnp.bfloat16, jnp.float32
SLOTS, ROWS, D = 8, 24, 8192
PAIR, HALF = 2 * ROWS, D // 2
TOK = SLOTS * ROWS
SEQ_ROWS = 12
HEADS = 4
QC, KC = 512, 128
PIECES, PIECE, SLICE = 5, 256, 512
SCALE = HD ** (-0.5)
MESH_ID = pl.DeviceIdType.MESH
MIB = 1024 * 1024


def place():
    dp, tensor = lax.axis_index("dp"), lax.axis_index("tensor")
    core, chip = lax.rem(dp, 2), dp // 2
    z, xh = lax.rem(chip, 4), chip // 4
    y, xl = tensor // 2, lax.rem(tensor, 2)
    here = dict(z=z, xh=xh, core=core, y=y, xl=xl, dp=dp, tensor=tensor)

    def along_z(at, cross=0):
        return ((xh * 4 + at) * 2 + lax.rem(core + cross, 2), tensor)

    def along_y(at):
        return (dp, at * 2 + xl)

    here["z_up"] = along_z(lax.rem(z + 1, 4))
    here["z_down"] = along_z(lax.rem(z + 3, 4))
    here["z_up_cross"] = along_z(lax.rem(z + 1, 4), 1)
    here["z_down_cross"] = along_z(lax.rem(z + 3, 4), 1)
    here["pass_from"] = lax.rem(z + 3 + 2 * core, 4)
    here["pass_to"] = along_z(lax.rem(z + 1 + 2 * core, 4))
    here["y_up"] = along_y(lax.rem(y + 1, 4))
    here["y_down"] = along_y(lax.rem(y + 3, 4))
    here["x_lo"] = (dp, y * 2 + 1 - xl)
    here["x_hi"] = (((1 - xh) * 4 + z) * 2 + core, tensor)
    here["x_hi_cross"] = (((1 - xh) * 4 + z) * 2 + 1 - core, tensor)
    here["sibling"] = (chip * 2 + 1 - core, tensor)
    here["z_even"] = along_z(z + 1 - 2 * lax.rem(z, 2))
    here["z_odd"] = along_z(3 - z)
    here["y_even"] = along_y(y + 1 - 2 * lax.rem(y, 2))
    here["y_odd"] = along_y(3 - y)
    return here


def greet(devices):
    barrier = pltpu.get_barrier_semaphore()
    for device in devices:
        pl.semaphore_signal(barrier, inc=1, device_id=device, device_id_type=MESH_ID)
    pl.semaphore_wait(barrier, len(devices))


def remote(src, dst, send, recv, device):
    return pltpu.make_async_remote_copy(
        src_ref=src, dst_ref=dst, send_sem=send, recv_sem=recv, device_id=device, device_id_type=MESH_ID
    )


def dot(a, b, ca=1, cb=0):
    return lax.dot_general(a, b, (((ca,), (cb,)), ((), ())), preferred_element_type=F32)


def cols(at, width=SLICE):
    return pl.ds(pl.multiple_of(at * width, width), width)


def layer_kernel(
    hidden, cot, gain, w_query, w_key, w_value, w_out, cosine, sine, bias,
    layer_out, input_grad, query_share, key_share, value_share, out_share, gain_out,
    wq, wkv, wo, rows_n, rows_c, flat_n, flat_c, got_n, got_c, passed, mixed, grads,
    t_far_r, t_side_r, t_near_r, t_pair_r, far_r, side_r, near_r, pair_r,
    gain_s, gain_r, query_acc, kv_acc, query_rot, key_rot, values, grad_mixed, probs,
    inverse, summed,
    w_sems, wo_sems, a_send, a_recv, f_recv, s_send, s_recv, p_recv, own_sems, c_send, c_recv, h_send, h_recv, m_send, m_recv,
    d_send, d_recv, j_send, j_recv, t_send, t_recv, g_send, g_recv,
):
    here = place()
    y, xl, z, xh, core = here["y"], here["xl"], here["z"], here["xh"], here["core"]
    y_up, y_down, y_far = lax.rem(y + 1, 4), lax.rem(y + 3, 4), lax.rem(y + 2, 4)
    z_up, z_down, z_far = lax.rem(z + 1, 4), lax.rem(z + 3, 4), lax.rem(z + 2, 4)
    own, mate = here["tensor"], y * 2 + 1 - xl
    toward = ((here["y_up"], y_up), (here["y_down"], y_down))
    toward_z = ((here["z_up"], z_up), (here["z_down"], z_down))
    rows = (rows_n, rows_c)

    loads = (
        pltpu.make_async_copy(w_query, wq, w_sems.at[0]),
        pltpu.make_async_copy(w_key, wkv.at[:, pl.ds(0, KC)], w_sems.at[1]),
        pltpu.make_async_copy(w_value, wkv.at[:, pl.ds(KC, KC)], w_sems.at[2]),
    )

    def load_out(b):
        half, block = b // 16, lax.rem(b, 16)
        return pltpu.make_async_copy(w_out.at[cols(half, PIECE), cols(block)], wo.at[b], wo_sems.at[b])

    for copy in loads:
        copy.start()

    @pl.loop(0, 32)
    def _(b):
        load_out(b).start()

    def mine(ref, at):
        return ref[:, at].astype(F32)

    def give(ref, at, block):
        ref[:, at] = block.astype(BF)

    def square(i, total):
        block = mine(hidden, cols(i))
        return total + jnp.sum(block * block, axis=1, keepdims=True)

    mean = lax.fori_loop(0, 16, square, jnp.zeros((ROWS, 1), F32)) / D
    inverse[...] = jnp.broadcast_to(lax.rsqrt(mean + EPS), (ROWS, 128))

    @pl.loop(0, 8)
    def _(k):
        scale = inverse[:, :1]
        normed = [
            mine(hidden, cols(2 * k + p)) * scale * gain[:, cols(2 * k + p)] for p in range(2)
        ]
        rows_n[own, :, cols(k)] = jnp.concatenate(normed, axis=0).astype(BF)
        rows_c[own, :, cols(k)] = jnp.concatenate(
            [mine(cot, cols(2 * k + p)) for p in range(2)], axis=0
        ).astype(BF)

    greet([here[name] for name in (
        "y_up", "y_down", "x_lo", "z_up", "z_down", "z_up_cross", "z_down_cross", "x_hi", "x_hi_cross", "sibling",
    )])

    pushed = ([], [])

    def push(a, number, slot, device):
        copy = remote(rows[a].at[slot], rows[a].at[slot], a_send.at[a, number], a_recv.at[a, slot], device)
        copy.start()
        pushed[a].append(copy)

    def landed(a, slot):
        remote(rows[a].at[slot], rows[a].at[slot], a_send.at[a, 0], a_recv.at[a, slot], here["x_lo"]).wait_recv()

    def push_own(a):
        push(a, 0, own, here["x_lo"])
        push(a, 1, own, here["y_up"])
        push(a, 2, own, here["y_down"])

    def push_mate(a):
        landed(a, mate)
        push(a, 3, mate, here["y_up"])
        push(a, 4, mate, here["y_down"])

    halves = (pl.ds(0, HALF // 2), pl.ds(HALF // 2, HALF // 2))

    def far_copy(a, way):
        slot = (y_down, y_up)[way] * 2 + xl
        ref = rows[a].at[slot, :, halves[way]]
        return remote(ref, ref, a_send.at[a, 5 + way], f_recv.at[a, way], toward[way][0])

    def push_far(a):
        for way in range(2):
            landed(a, (y_down, y_up)[way] * 2 + xl)
            copy = far_copy(a, way)
            copy.start()
            pushed[a].append(copy)

    def push_last(a):
        slot = y_far * 2 + xl
        for way in range(2):
            ref = rows[a].at[slot, :, halves[way]]
            remote(ref, ref, a_send.at[a, 0], f_recv.at[a, way], here["x_lo"]).wait_recv()
        push(a, 7, slot, here["x_lo"])

    def rest(a):
        landed(a, y_down * 2 + 1 - xl)
        landed(a, y_up * 2 + 1 - xl)
        landed(a, y_far * 2 + 1 - xl)

    def flatten(a, k):
        chunks = [rows[a][slot, :, cols(k)].astype(F32) for slot in range(SLOTS)]
        return [
            jnp.concatenate([c[p * ROWS : (p + 1) * ROWS] for c in chunks], axis=0).astype(BF) for p in range(2)
        ]

    def slice_copy(number):
        cross = 1 - core
        src, dst, recv, device = (
            (flat_n.at[core, z_far], passed.at[0], p_recv.at[0], "z_up"),
            (flat_n.at[cross, z_far], passed.at[1], p_recv.at[1], "z_down"),
            (flat_n.at[core, z_up], got_n.at[z, core], s_recv.at[z, core], "z_up"),
            (flat_n.at[core, z_down], got_n.at[z, core], s_recv.at[z, core], "z_down"),
            (flat_n.at[cross, z_up], got_n.at[z, core], s_recv.at[z, core], "z_up_cross"),
            (flat_n.at[cross, z_down], got_n.at[z, core], s_recv.at[z, core], "z_down_cross"),
            (flat_n.at[cross, z], got_n.at[z, core], s_recv.at[z, core], "sibling"),
            (passed.at[0], got_n.at[z_down, core], s_recv.at[z_down, core], "z_up"),
            (passed.at[1], got_n.at[z_up, core], s_recv.at[z_up, core], "z_down_cross"),
        )[number]
        return remote(src, dst, s_send.at[number], recv, here[device])

    def own_slice():
        return pltpu.make_async_copy(flat_n.at[core, z], got_n.at[z, core], own_sems.at[0])

    def slices_start():
        for number in range(7):
            slice_copy(number).start()
        own_slice().start()

    def slices_pass():
        for number in range(2):
            slice_copy(number).wait_recv()
            slice_copy(7 + number).start()

    def slices_wait():
        own_slice().wait()
        for at, cross in ((0, 1), (1, 0), (1, 1), (2, 0), (2, 1), (3, 0), (3, 1)):
            zs, cs = lax.rem(z + at, 4), lax.rem(core + cross, 2)
            ref = got_n.at[zs, cs]
            remote(ref, ref, s_send.at[0], s_recv.at[zs, cs], here["sibling"]).wait_recv()

    def cot_copy(number):
        cross = 1 - core
        src, device = (
            (flat_c.at[core, 1 - xh], "x_hi"), (flat_c.at[cross, 1 - xh], "x_hi_cross"),
            (flat_c.at[cross, xh], "sibling"),
        )[number]
        return remote(src, got_c.at[xh, core], c_send.at[number], c_recv.at[xh, core], here[device])

    def own_cot():
        return pltpu.make_async_copy(flat_c.at[core, xh], got_c.at[xh, core], own_sems.at[1])

    def mix_copy(number):
        device = ("x_hi", "x_hi_cross", "sibling")[number]
        ref = mixed.at[xh, core]
        return remote(ref, ref, h_send.at[number], h_recv.at[xh, core], here[device])

    def cross_wait():
        own_cot().wait()
        for xs, cs in ((xh, 1 - core), (1 - xh, core), (1 - xh, 1 - core)):
            ref = got_c.at[xs, cs]
            remote(ref, ref, c_send.at[0], c_recv.at[xs, cs], here["sibling"]).wait_recv()
            ref = mixed.at[xs, cs]
            remote(ref, ref, h_send.at[0], h_recv.at[xs, cs], here["sibling"]).wait_recv()

    def columns_copy(number):
        at, device = (
            (z, "sibling"), (z, "z_up"), (z, "z_down"), (z_down, "sibling"), (z_up, "sibling"),
            (here["pass_from"], "pass_to"), (z_far, "sibling"),
        )[number]
        ref = grads.at[at, core]
        return remote(ref, ref, m_send.at[number], m_recv.at[at, core], here[device])

    def columns_got(zs, cs):
        ref = grads.at[zs, cs]
        remote(ref, ref, m_send.at[0], m_recv.at[zs, cs], here["sibling"]).wait_recv()

    def columns_start():
        for number in (1, 2, 0):
            columns_copy(number).start()

    def columns_pass():
        columns_got(z_down, core)
        columns_got(z_up, core)
        for number in (5, 3, 4):
            columns_copy(number).start()

    def columns_last():
        columns_got(z_far, core)
        columns_copy(6).start()

    def columns_wait():
        for zs in range(4):
            columns_got(zs, 1 - core)

    push_own(0)
    push_mate(0)
    push_far(0)
    push_own(1)
    push_last(0)
    rest(0)

    query_acc[...] = jnp.zeros_like(query_acc)
    kv_acc[...] = jnp.zeros_like(kv_acc)
    for copy in loads:
        copy.wait()

    @pl.loop(0, 8)
    def _(k):
        for p, block in enumerate(flatten(0, k)):
            flat_n[p, lax.rem(k, 4), k // 4] = block
            query_acc[...] += dot(block, wq[cols(2 * k + p), :])
            kv_acc[...] += dot(block, wkv[cols(2 * k + p), :])

    slices_start()
    push_mate(1)

    def rotated(u):
        return u * cosine[...] + pltpu.roll(u, HD // 2, 1) * sine[...]

    def unrotated(g):
        return g * cosine[...] - pltpu.roll(g, HD // 2, 1) * sine[...]

    def head(h):
        return slice(h * HD, (h + 1) * HD)

    key_rot[...] = rotated(kv_acc[:, :HD]).astype(BF)
    values[...] = kv_acc[:, HD:].astype(BF)
    for h in range(HEADS):
        query_rot[:, head(h)] = rotated(query_acc[:, head(h)]).astype(BF)
    for h in range(HEADS):
        logits = dot(query_rot[:, head(h)], key_rot[...], 1, 1) * SCALE + bias[...]
        powers = jnp.exp(logits - jnp.max(logits, axis=1, keepdims=True))
        prob = powers / jnp.sum(powers, axis=1, keepdims=True)
        probs[h] = prob
        mixed[xh, core, :, head(h)] = dot(prob.astype(BF), values[...]).astype(BF)
    push_far(1)
    for number in range(3):
        mix_copy(number).start()

    @pl.loop(0, 32)
    def _(b):
        load_out(b).wait()

    for copy in pushed[0]:
        copy.wait_send()

    def to_chunks(a, k, blocks):
        for slot in range(SLOTS):
            rows[a][slot, :, cols(k)] = jnp.concatenate(
                [b[slot * ROWS : (slot + 1) * ROWS] for b in blocks], axis=0
            ).astype(BF)

    @pl.loop(0, 8)
    def _(k):
        to_chunks(0, k, [
            dot(mixed[xh, core, :, :PIECE], wo[2 * k + p]) + dot(mixed[xh, core, :, PIECE:], wo[16 + 2 * k + p]) for p in range(2)
        ])

    def t_copy(kind, a, way):
        device, at = toward[way]
        slot = (y_far * 2 + way, at * 2 + 1 - way, at * 2 + way)[kind]
        dst = (t_far_r, t_side_r, t_near_r)[kind].at[a, way]
        return remote(rows[a].at[slot], dst, t_send.at[kind, a, way], t_recv.at[kind, a, way], device)

    def t_start(a):
        for kind in range(2):
            for way in range(2):
                t_copy(kind, a, way).start()

    def t_relay(a):
        for way in range(2):
            t_copy(0, a, way).wait()
            slot = toward[way][1] * 2 + way

            @pl.loop(0, 8)
            def _(k, way=way, slot=slot):
                rows[a][slot, :, cols(k)] = (
                    rows[a][slot, :, cols(k)].astype(F32) + t_far_r[a, way, :, cols(k)].astype(F32)
                ).astype(BF)

            t_copy(2, a, way).start()

    def t_total(a, side, k):
        return (
            rows[a][y * 2 + side, :, cols(k)].astype(F32)
            + t_side_r[a, 1 - side, :, cols(k)].astype(F32)
            + t_near_r[a, side, :, cols(k)].astype(F32)
        )

    def t_pair(a):
        return remote(rows[a].at[mate], t_pair_r.at[a], t_send.at[3, a, 0], t_recv.at[3, a, 0], here["x_lo"])

    def t_settle(a):
        for way in range(2):
            t_copy(1, a, way).wait()
            t_copy(2, a, way).wait()

        @pl.loop(0, 8)
        def _(k):
            rows[a][mate, :, cols(k)] = t_total(a, 1 - xl, k).astype(BF)

        t_pair(a).start()

    push_last(1)
    t_start(0)
    rest(1)

    query_acc[...] = jnp.zeros_like(query_acc)

    @pl.loop(0, 8)
    def _(k):
        for p, block in enumerate(flatten(1, k)):
            flat_c[p, k // 4, lax.rem(k, 4)] = block
            for half in range(2):
                query_acc[:, half * PIECE : (half + 1) * PIECE] += dot(block, wo[half * 16 + 2 * k + p], 1, 1)

    for number in range(3):
        cot_copy(number).start()
    own_cot().start()
    slices_pass()
    grad_mixed[...] = query_acc[...].astype(BF)

    def joint(p, side):
        total = jnp.zeros((PIECE, SLICE), F32)
        for zs in range(4):
            for cs in range(2):
                total += dot(grads[zs, cs, :, p * PIECE : (p + 1) * PIECE], got_n[zs, cs, side], 0, 0)
        return total

    def joint_pair(p):
        return remote(wo.at[p], pair_r.at[p], j_send.at[p], j_recv.at[p], here["x_hi"])

    def outer(p, at):
        total = jnp.zeros((PIECE, SLICE), F32)
        for xs in range(2):
            for cs in range(2):
                total += dot(mixed[xs, cs, :, p * PIECE : (p + 1) * PIECE], got_c[xs, cs, at], 0, 0)
        return total

    def d_copy(kind, way):
        dst = (far_r, side_r, near_r)[kind].at[way]
        return remote(wo.at[3 + kind * 2 + way], dst, d_send.at[kind, way], d_recv.at[kind, way], toward_z[way][0])

    t_relay(0)

    dkey = jnp.zeros((TOK, HD), F32)
    dvalues = jnp.zeros((TOK, HD), F32)
    for h in range(HEADS):
        prob = probs[h]
        grad = grad_mixed[:, head(h)]
        dvalues += dot(prob.astype(BF), grad, 0, 0)
        prob_grad = dot(grad, values[...], 1, 1)
        row_delta = jnp.sum(prob * prob_grad, axis=1, keepdims=True)
        score_grad = (prob * (prob_grad - row_delta) * SCALE).astype(BF)
        grads[z, core, :, head(h)] = unrotated(dot(score_grad, key_rot[...])).astype(BF)
        dkey += dot(score_grad, query_rot[:, head(h)], 0, 0)
    grads[z, core, :, QC : QC + HD] = unrotated(dkey).astype(BF)
    grads[z, core, :, QC + HD :] = dvalues.astype(BF)
    columns_start()

    for copy in pushed[1]:
        copy.wait_send()

    @pl.loop(0, 8)
    def _(k):
        blocks = []
        for p in range(2):
            at = 2 * k + p
            block = dot(grads[z, core, :, :QC], wq[cols(at), :], 1, 1)
            block += dot(grads[z, core, :, QC:], wkv[cols(at), :], 1, 1)
            blocks.append(block)
            terms = block.astype(BF).astype(F32) * flat_n[p, lax.rem(k, 4), k // 4].astype(F32)
            gain_s[0, pl.ds(at, 1), :] = jnp.sum(terms, axis=0, keepdims=True) / gain[:, cols(at)]
        to_chunks(1, k, blocks)

    t_start(1)

    ways = ("sibling", "y_even", "y_odd", "x_lo", "z_even", "z_odd", "x_hi")

    def g_copy(step):
        return remote(gain_s.at[step], gain_r.at[step], g_send.at[step], g_recv.at[step], here[ways[step]])

    def gain_step(step):
        if step:
            g_copy(step - 1).wait()
            gain_s[step] = gain_s[step - 1] + gain_r[step - 1]
        if step < 7:
            g_copy(step).start()

    gain_step(0)
    columns_pass()
    cross_wait()
    for way in range(2):
        wo[3 + way] = outer(way, z_far).astype(BF)
        d_copy(0, way).start()
    for way in range(2):
        wo[5 + way] = outer(1 - way, toward_z[way][1]).astype(BF)
        d_copy(1, way).start()
    gain_step(1)
    t_settle(0)
    columns_last()
    t_relay(1)
    gain_step(2)
    for way in range(2):
        block = outer(way, toward_z[way][1])
        d_copy(0, way).wait()
        wo[7 + way] = (block + far_r[way].astype(F32)).astype(BF)
        d_copy(2, way).start()
    slices_wait()
    columns_wait()
    for p in range(3):
        wo[p] = joint(p, 1 - xh).astype(BF)
        joint_pair(p).start()
    gain_step(3)
    t_settle(1)
    gain_step(4)
    t_pair(0).wait()

    @pl.loop(0, 8)
    def _(k):
        total = t_total(0, xl, k) + t_pair_r[0, :, cols(k)].astype(F32)
        for p in range(2):
            at = cols(2 * k + p)
            give(layer_out, at, mine(hidden, at) + total[p * ROWS : (p + 1) * ROWS])

    gain_step(5)
    gain_step(6)
    t_pair(1).wait()
    scale = inverse[:, :1]

    def weigh(k, total):
        block = t_total(1, xl, k) + t_pair_r[1, :, cols(k)].astype(F32)
        summed[:, cols(k)] = block
        for p in range(2):
            at = cols(2 * k + p)
            scaled = mine(hidden, at) * scale
            weighted = block[p * ROWS : (p + 1) * ROWS] * gain[:, at]
            total = total + jnp.sum(weighted * scaled, axis=1, keepdims=True)
        return total

    mean = lax.fori_loop(0, 8, weigh, jnp.zeros((ROWS, 1), F32)) / D

    @pl.loop(0, 8)
    def _(k):
        block = summed[:, cols(k)]
        for p in range(2):
            at = cols(2 * k + p)
            scaled = mine(hidden, at) * scale
            weighted = block[p * ROWS : (p + 1) * ROWS] * gain[:, at]
            give(input_grad, at, mine(cot, at) + scale * (weighted - scaled * mean))

    gain_step(7)
    gain_out[...] = gain_s[7, pl.ds(here["dp"], 1), :]

    for p in range(2):
        total = outer(p, z)
        d_copy(1, 1 - p).wait()
        d_copy(2, p).wait()
        out_share[p * PIECE : (p + 1) * PIECE, :] = (
            total + side_r[1 - p].astype(F32) + near_r[p].astype(F32)
        )
    for p in range(3):
        total = joint(p, xh)
        joint_pair(p).wait()
        total = (total + pair_r[p].astype(F32)).T
        if p < 2:
            query_share[:, p * PIECE : (p + 1) * PIECE] = total
        else:
            key_share[...] = total[:, :KC]
            value_share[...] = total[:, KC:]
    for number in range(9):
        slice_copy(number).wait_send()
    for number in range(7):
        columns_copy(number).wait_send()
    for number in range(3):
        cot_copy(number).wait_send()
        mix_copy(number).wait_send()


def copy_kernel(*refs):
    count = len(refs) // 2
    for i in range(count):
        refs[count + i][...] = refs[i][...]


def results(arrays):
    at_vmem = pl.BlockSpec(memory_space=pltpu.VMEM)
    return pl.pallas_call(
        copy_kernel,
        out_shape=tuple(jax.ShapeDtypeStruct(a.shape, a.dtype) for a in arrays),
        in_specs=[at_vmem] * len(arrays),
        out_specs=tuple([at_vmem] * len(arrays)),
    )(*arrays)


def tables(own_len):
    token = np.arange(TOK)
    seq = token % 2
    pos = (token // ROWS) * own_len + token % ROWS // 2
    frequency = ROPE_BASE ** (-2.0 * np.arange(HD // 2) / HD)
    angles = pos[:, None] * frequency[None, :]
    cosine = np.concatenate([np.cos(angles), np.cos(angles)], axis=1).astype(np.float32)
    sine = np.concatenate([-np.sin(angles), np.sin(angles)], axis=1).astype(np.float32)
    allowed = (seq[:, None] == seq[None, :]) & (pos[:, None] >= pos[None, :])
    return cosine, sine, np.where(allowed, 0.0, -1e30).astype(np.float32)


def shards(hidden_in, norm_gain, w_query, w_key, w_value, w_out, cotangent):
    dma, vmem = pltpu.SemaphoreType.DMA, pltpu.VMEM
    chunk = (PAIR, HALF)
    block = (PIECE, SLICE)
    at_vmem = pl.BlockSpec(memory_space=pltpu.VMEM)
    at_any = pl.BlockSpec(memory_space=pl.ANY)
    shape = jax.ShapeDtypeStruct
    cosine, sine, bias = tables(SEQ_ROWS)
    own_shape = (ROWS, D)

    def rows_of(array):
        return array.transpose(1, 0, 2).reshape(ROWS, D)

    def as_given(array):
        return array.reshape(SEQ_ROWS, 2, D).transpose(1, 0, 2)

    layer_out, input_grad, query_share, key_share, value_share, out_share, gain_total = pl.pallas_call(
        layer_kernel,
        out_shape=(
            shape(own_shape, BF), shape(own_shape, BF), shape((SLICE, QC), F32), shape((SLICE, KC), F32),
            shape((SLICE, KC), F32), shape((QC, SLICE), F32), shape((1, SLICE), F32),
        ),
        in_specs=[at_vmem] * 3 + [at_any] * 4 + [at_vmem] * 3,
        out_specs=tuple([at_vmem] * 7),
        scratch_shapes=[
            vmem((D, QC), BF), vmem((D, 2 * KC), BF), vmem((32,) + block, BF),
            vmem((SLOTS,) + chunk, BF), vmem((SLOTS,) + chunk, BF),
            vmem((2, 4, 2, TOK, SLICE), BF), vmem((2, 2, 4, TOK, SLICE), BF),
            vmem((4, 2, 2, TOK, SLICE), BF), vmem((2, 2, 4, TOK, SLICE), BF),
            vmem((2, 2, TOK, SLICE), BF), vmem((2, 2, TOK, QC), BF), vmem((4, 2, TOK, QC + 2 * KC), BF),
            vmem((2, 2) + chunk, BF), vmem((2, 2) + chunk, BF), vmem((2, 2) + chunk, BF), vmem((2,) + chunk, BF),
            vmem((2,) + block, BF), vmem((2,) + block, BF), vmem((2,) + block, BF), vmem((3,) + block, BF),
            vmem((8, 16, SLICE), F32), vmem((7, 16, SLICE), F32),
            vmem((TOK, QC), F32), vmem((TOK, 2 * KC), F32),
            vmem((TOK, QC), BF), vmem((TOK, HD), BF), vmem((TOK, HD), BF),
            vmem((TOK, QC), BF),
            vmem((HEADS, TOK, TOK), F32), vmem((ROWS, 128), F32), vmem(chunk, F32),
            dma((3,)), dma((32,)), dma((2, 8)), dma((2, SLOTS)), dma((2, 2)), dma((9,)), dma((4, 2)), dma((2,)), dma((2,)),
            dma((3,)), dma((2, 2)), dma((3,)), dma((2, 2)), dma((7,)), dma((4, 2)),
            dma((3, 2)), dma((3, 2)), dma((3,)), dma((3,)), dma((4, 2, 2)), dma((4, 2, 2)), dma((7,)), dma((7,)),
        ],
        compiler_params=pltpu.CompilerParams(
            collective_id=0, has_side_effects=True, vmem_limit_bytes=62 * MIB
        ),
    )(
        rows_of(hidden_in), rows_of(cotangent), norm_gain.reshape(1, D),
        w_query, w_key, w_value, w_out, jnp.asarray(cosine), jnp.asarray(sine), jnp.asarray(bias),
    )
    share = D // 128
    gain_share = lax.dynamic_slice_in_dim(gain_total.reshape(SLICE), lax.axis_index("tensor") * share, share, 0)
    return (as_given(layer_out), as_given(input_grad)) + results(
        (query_share, key_share, value_share, out_share)
    ) + (gain_share,)


def solution(mesh):
    return jax.shard_map(
        shards,
        mesh=mesh,
        in_specs=(
            P("dp", "tensor", None), P(), P(None, "tensor"), P(None, "tensor"), P(None, "tensor"),
            P("tensor", None), P("dp", "tensor", None),
        ),
        out_specs=(
            P("dp", "tensor", None), P("dp", "tensor", None), P("dp", "tensor"), P("dp", "tensor"),
            P("dp", "tensor"), P("tensor", "dp"), P(("dp", "tensor")),
        ),
        check_vma=False,
    )
```

time: 202 us -> 163 us (0.81)
  Pallas kernels: 183 us -> 153 us
  local copies, waits for them, and re-layouts: 17.9 us -> 9.04 us
    pallas_call x1 -> x2, Pallas kernels: 183 us -> 153 us  [the longest x1 149 us: shards(): pl.pallas_call(layer_kernel, out_shape=(shape(own_shape, BF), shape(own_s...]
    unnamed x9 -> x0, local copies, waits for them, and re-layouts: 13.4 us -> none
    reshape x4, local copies, waits for them, and re-layouts: 3.89 us -> 7.77 us  [the longest x2 3.99 us: as_given(): return array.reshape(SEQ_ROWS, 2, D).transpose(1, 0, 2)]
where the time goes in v2:
time: 163 us; the launch traced here: 162 us
  Pallas kernels  153 us (94%)
  local copies, waits for them, and re-layouts  9.04 us (6%)
    pallas_call x1, Pallas kernels, shards(): pl.pallas_call(layer_kernel, out_shape=(shape(own_shape, BF), shape(own_s...  149 us
    reshape x2, local copies, waits for them, and re-layouts, as_given(): return array.reshape(SEQ_ROWS, 2, D).transpose(1, 0, 2)  3.99 us
    reshape x2, local copies, waits for them, and re-layouts, rows_of(): return array.transpose(1, 0, 2).reshape(ROWS, D)  3.78 us

profile of v2, /device:TPU:1, one launch (start us, length us, event | category | flops | bytes accessed | tf_op | source)
XLA Modules:
  0.0 162.2 jit_solution(14988075740629091978)
XLA Ops:
  0.6 1.9 %reshape.31.hidden = bf16[24,8192]{1,0:T(8,128)(2,1)} reshape(bf16[12,2,8192]{2,1,0:T(2,128)(2,1)} %bitcast.7) | data formatting | bytes 786432 | tf_op jit(solution)/shard_map/reshape | solution.py:607
  2.5 1.9 %reshape.32.cot = bf16[24,8192]{1,0:T(8,128)(2,1)} reshape(bf16[12,2,8192]{2,1,0:T(2,128)(2,1)} %bitcast.8) | data formatting | bytes 786432 | tf_op jit(solution)/shard_map/reshape | solution.py:607
  4.4 149.3 %shard_map.153 = (bf16[24,8192]{1,0:T(8,128)(2,1)}, bf16[24,8192]{1,0:T(8,128)(2,1)}, f32[512,512]{1,0:T(8,128)}, f32[512,128]{1,0:T(8,128)}, f32[512,128]{1,0:T...) custom-call(bf16[24,8192]{1,0:T(8,128)(2,1)} %reshape.31.hidden, bf16[24,8192]{1,0:T(8,128)(2,1)} %reshape.32.cot, ...), custom_call_target="tpu_custom_call" | custom-call | tf_op jit(solution)/shard_map/pallas_call | solution.py:612
  153.8 1.3 dynamic-slice_bitcast_fusion
  155.0 2.0 %reshape.34 = bf16[12,2,8192]{2,1,0:T(2,128)(2,1)} reshape(bf16[24,8192]{1,0:T(8,128)(2,1)} %get-tuple-element.18) | data formatting | bytes 786432 | tf_op jit(solution)/shard_map/reshape | solution.py:610
  157.0 2.0 %reshape.35 = bf16[12,2,8192]{2,1,0:T(2,128)(2,1)} reshape(bf16[24,8192]{1,0:T(8,128)(2,1)} %get-tuple-element.19) | data formatting | bytes 786432 | tf_op jit(solution)/shard_map/reshape | solution.py:610
  159.0 3.2 %shard_map.154 = (f32[512,512]{1,0:T(8,128)}, f32[512,128]{1,0:T(8,128)}, f32[512,128]{1,0:T(8,128)}, f32[512,512]{1,0:T(8,128)}) custom-call(f32[512,512]{1,0:T(8,128)} %get-tuple-element.20.refs_0_, f32[512,128]{1,0:T(8,128)} %get-tuple-element.21.refs_1_, f32[512,128]{1,0:T(8,128)} %get-tuple-element.22.refs_2_, f32[512,512]{1,0:T(8,128)} %get-tuple-element.23.refs_3_), custom_call_target="tpu_custom_call" | custom-call | tf_op jit(solution)/shard_map/pallas_call | solution.py:576

commit v3 on v2

--- a/solution.py
+++ b/solution.py
@@ -47,10 +47,9 @@
     here["x_hi"] = (((1 - xh) * 4 + z) * 2 + core, tensor)
     here["x_hi_cross"] = (((1 - xh) * 4 + z) * 2 + 1 - core, tensor)
     here["sibling"] = (chip * 2 + 1 - core, tensor)
-    here["z_even"] = along_z(z + 1 - 2 * lax.rem(z, 2))
-    here["z_odd"] = along_z(3 - z)
-    here["y_even"] = along_y(y + 1 - 2 * lax.rem(y, 2))
-    here["y_odd"] = along_y(3 - y)
+    here["chip"] = chip
+    here["tensor_peers"] = [(dp, lax.rem(tensor + i, 8)) for i in range(1, 8)]
+    here["chip_peers"] = [(lax.rem(chip + i, 8) * 2 + core, tensor) for i in range(1, 8)]
     return here
 
 
@@ -80,8 +79,8 @@
     layer_out, input_grad, query_share, key_share, value_share, out_share, gain_out,
     wq, wkv, wo, rows_n, rows_c, flat_n, flat_c, got_n, got_c, passed, mixed, grads,
     t_far_r, t_side_r, t_near_r, t_pair_r, far_r, side_r, near_r, pair_r,
-    gain_s, gain_r, query_acc, kv_acc, query_rot, key_rot, values, grad_mixed, probs,
-    inverse, summed,
+    gain_own, gain_t, gain_c, gain_s, query_acc, kv_acc, query_rot, key_rot, values, grad_mixed, probs,
+    inverse, summed, joint_own,
     w_sems, wo_sems, a_send, a_recv, f_recv, s_send, s_recv, p_recv, own_sems, c_send, c_recv, h_send, h_recv, m_send, m_recv,
     d_send, d_recv, j_send, j_recv, t_send, t_recv, g_send, g_recv,
 ):
@@ -135,9 +134,10 @@
             [mine(cot, cols(2 * k + p)) for p in range(2)], axis=0
         ).astype(BF)
 
-    greet([here[name] for name in (
-        "y_up", "y_down", "x_lo", "z_up", "z_down", "z_up_cross", "z_down_cross", "x_hi", "x_hi_cross", "sibling",
-    )])
+    greet(
+        here["tensor_peers"] + here["chip_peers"]
+        + [here[name] for name in ("z_up_cross", "z_down_cross", "x_hi_cross", "sibling")]
+    )
 
     pushed = ([], [])
 
@@ -149,8 +149,10 @@
     def landed(a, slot):
         remote(rows[a].at[slot], rows[a].at[slot], a_send.at[a, 0], a_recv.at[a, slot], here["x_lo"]).wait_recv()
 
-    def push_own(a):
+    def push_over(a):
         push(a, 0, own, here["x_lo"])
+
+    def push_along(a):
         push(a, 1, own, here["y_up"])
         push(a, 2, own, here["y_down"])
 
@@ -167,6 +169,12 @@
         return remote(ref, ref, a_send.at[a, 5 + way], f_recv.at[a, way], toward[way][0])
 
     def push_far(a):
+        if a:
+            landed(a, y_down * 2)
+            push(a, 5, y_down * 2, here["y_up"])
+            landed(a, y_up * 2 + 1)
+            push(a, 6, y_up * 2 + 1, here["y_down"])
+            return
         for way in range(2):
             landed(a, (y_down, y_up)[way] * 2 + xl)
             copy = far_copy(a, way)
@@ -181,9 +189,11 @@
         push(a, 7, slot, here["x_lo"])
 
     def rest(a):
-        landed(a, y_down * 2 + 1 - xl)
-        landed(a, y_up * 2 + 1 - xl)
+        landed(a, y_down * 2 + (1 if a else 1 - xl))
+        landed(a, y_up * 2 + (0 if a else 1 - xl))
         landed(a, y_far * 2 + 1 - xl)
+        if a:
+            landed(a, y_far * 2 + xl)
 
     def flatten(a, k):
         chunks = [rows[a][slot, :, cols(k)].astype(F32) for slot in range(SLOTS)]
@@ -209,11 +219,6 @@
     def own_slice():
         return pltpu.make_async_copy(flat_n.at[core, z], got_n.at[z, core], own_sems.at[0])
 
-    def slices_start():
-        for number in range(7):
-            slice_copy(number).start()
-        own_slice().start()
-
     def slices_pass():
         for number in range(2):
             slice_copy(number).wait_recv()
@@ -280,11 +285,14 @@
         for zs in range(4):
             columns_got(zs, 1 - core)
 
-    push_own(0)
+    push_over(0)
+    push_along(0)
     push_mate(0)
     push_far(0)
-    push_own(1)
+    push_over(1)
     push_last(0)
+    push_along(1)
+    push_mate(1)
     rest(0)
 
     query_acc[...] = jnp.zeros_like(query_acc)
@@ -292,15 +300,18 @@
     for copy in loads:
         copy.wait()
 
-    @pl.loop(0, 8)
-    def _(k):
-        for p, block in enumerate(flatten(0, k)):
-            flat_n[p, lax.rem(k, 4), k // 4] = block
-            query_acc[...] += dot(block, wq[cols(2 * k + p), :])
-            kv_acc[...] += dot(block, wkv[cols(2 * k + p), :])
-
-    slices_start()
-    push_mate(1)
+    for step, at in enumerate((z_far, z_up, z_down, z)):
+        @pl.loop(0, 2)
+        def _(side, at=at):
+            k = side * 4 + at
+            for p, block in enumerate(flatten(0, k)):
+                flat_n[p, at, side] = block
+                query_acc[...] += dot(block, wq[cols(2 * k + p), :])
+                kv_acc[...] += dot(block, wkv[cols(2 * k + p), :])
+
+        for number in ((0, 1), (2, 4), (3, 5), (6,))[step]:
+            slice_copy(number).start()
+    own_slice().start()
 
     def rotated(u):
         return u * cosine[...] + pltpu.roll(u, HD // 2, 1) * sine[...]
@@ -321,7 +332,6 @@
         prob = powers / jnp.sum(powers, axis=1, keepdims=True)
         probs[h] = prob
         mixed[xh, core, :, head(h)] = dot(prob.astype(BF), values[...]).astype(BF)
-    push_far(1)
     for number in range(3):
         mix_copy(number).start()
 
@@ -389,23 +399,25 @@
 
         t_pair(a).start()
 
-    push_last(1)
+    push_far(1)
     t_start(0)
+    slices_pass()
     rest(1)
 
     query_acc[...] = jnp.zeros_like(query_acc)
 
-    @pl.loop(0, 8)
-    def _(k):
-        for p, block in enumerate(flatten(1, k)):
-            flat_c[p, k // 4, lax.rem(k, 4)] = block
-            for half in range(2):
-                query_acc[:, half * PIECE : (half + 1) * PIECE] += dot(block, wo[half * 16 + 2 * k + p], 1, 1)
-
-    for number in range(3):
-        cot_copy(number).start()
+    for step, side in enumerate((1 - xh, xh)):
+        @pl.loop(0, 4)
+        def _(at, side=side):
+            k = side * 4 + at
+            for p, block in enumerate(flatten(1, k)):
+                flat_c[p, side, at] = block
+                for half in range(2):
+                    query_acc[:, half * PIECE : (half + 1) * PIECE] += dot(block, wo[half * 16 + 2 * k + p], 1, 1)
+
+        for number in ((0, 1), (2,))[step]:
+            cot_copy(number).start()
     own_cot().start()
-    slices_pass()
     grad_mixed[...] = query_acc[...].astype(BF)
 
     def joint(p, side):
@@ -428,8 +440,6 @@
     def d_copy(kind, way):
         dst = (far_r, side_r, near_r)[kind].at[way]
         return remote(wo.at[3 + kind * 2 + way], dst, d_send.at[kind, way], d_recv.at[kind, way], toward_z[way][0])
-
-    t_relay(0)
 
     dkey = jnp.zeros((TOK, HD), F32)
     dvalues = jnp.zeros((TOK, HD), F32)
@@ -445,6 +455,7 @@
     grads[z, core, :, QC : QC + HD] = unrotated(dkey).astype(BF)
     grads[z, core, :, QC + HD :] = dvalues.astype(BF)
     columns_start()
+    t_relay(0)
 
     for copy in pushed[1]:
         copy.wait_send()
@@ -458,25 +469,50 @@
             block += dot(grads[z, core, :, QC:], wkv[cols(at), :], 1, 1)
             blocks.append(block)
             terms = block.astype(BF).astype(F32) * flat_n[p, lax.rem(k, 4), k // 4].astype(F32)
-            gain_s[0, pl.ds(at, 1), :] = jnp.sum(terms, axis=0, keepdims=True) / gain[:, cols(at)]
+            term = jnp.sum(terms, axis=0, keepdims=True) / gain[:, cols(at)]
+            for quarter in range(4):
+                gain_own[quarter, pl.ds(at, 1), :] = term[:, quarter * 128 : (quarter + 1) * 128]
         to_chunks(1, k, blocks)
 
+    def gain_over(number):
+        at = lax.rem(own + 1 + number, 8) // 2
+        return remote(
+            gain_own.at[at], gain_t.at[own], g_send.at[0, number], g_recv.at[0, own], here["tensor_peers"][number]
+        )
+
+    def gain_sibling():
+        return remote(gain_s.at[0], gain_s.at[1], g_send.at[1, 0], g_recv.at[1, 0], here["sibling"])
+
+    def gain_chips(number):
+        return remote(
+            gain_s.at[2], gain_c.at[here["chip"]], g_send.at[2, number], g_recv.at[2, here["chip"]],
+            here["chip_peers"][number],
+        )
+
+    def gain_sum(level, ref, mine, value):
+        ref[mine] = value
+        for i in range(1, 8):
+            at = lax.rem(mine + i, 8)
+            remote(ref.at[at], ref.at[at], g_send.at[level, 0], g_recv.at[level, at], here["sibling"]).wait_recv()
+        total = ref[0]
+        for i in range(1, 8):
+            total = total + ref[i]
+        return total
+
+    for number in range(7):
+        gain_over(number).start()
     t_start(1)
-
-    ways = ("sibling", "y_even", "y_odd", "x_lo", "z_even", "z_odd", "x_hi")
-
-    def g_copy(step):
-        return remote(gain_s.at[step], gain_r.at[step], g_send.at[step], g_recv.at[step], here[ways[step]])
-
-    def gain_step(step):
-        if step:
-            g_copy(step - 1).wait()
-            gain_s[step] = gain_s[step - 1] + gain_r[step - 1]
-        if step < 7:
-            g_copy(step).start()
-
-    gain_step(0)
     columns_pass()
+    t_settle(0)
+    columns_last()
+    t_relay(1)
+    slices_wait()
+    columns_wait()
+    for p in range(3):
+        wo[p] = joint(p, 1 - xh).astype(BF)
+        joint_pair(p).start()
+    gain_s[0] = gain_sum(0, gain_t, own, gain_own[y])
+    gain_sibling().start()
     cross_wait()
     for way in range(2):
         wo[3 + way] = outer(way, z_far).astype(BF)
@@ -484,24 +520,20 @@
     for way in range(2):
         wo[5 + way] = outer(1 - way, toward_z[way][1]).astype(BF)
         d_copy(1, way).start()
-    gain_step(1)
-    t_settle(0)
-    columns_last()
-    t_relay(1)
-    gain_step(2)
+    gain_sibling().wait()
+    gain_s[2] = gain_s[0] + gain_s[1]
+    for number in range(7):
+        gain_chips(number).start()
+    t_settle(1)
     for way in range(2):
         block = outer(way, toward_z[way][1])
         d_copy(0, way).wait()
         wo[7 + way] = (block + far_r[way].astype(F32)).astype(BF)
         d_copy(2, way).start()
-    slices_wait()
-    columns_wait()
     for p in range(3):
-        wo[p] = joint(p, 1 - xh).astype(BF)
-        joint_pair(p).start()
-    gain_step(3)
-    t_settle(1)
-    gain_step(4)
+        joint_own[p] = joint(p, xh)
+    for p in range(2):
+        out_share[p * PIECE : (p + 1) * PIECE, :] = outer(p, z)
     t_pair(0).wait()
 
     @pl.loop(0, 8)
@@ -511,8 +543,6 @@
             at = cols(2 * k + p)
             give(layer_out, at, mine(hidden, at) + total[p * ROWS : (p + 1) * ROWS])
 
-    gain_step(5)
-    gain_step(6)
     t_pair(1).wait()
     scale = inverse[:, :1]
 
@@ -537,25 +567,24 @@
             weighted = block[p * ROWS : (p + 1) * ROWS] * gain[:, at]
             give(input_grad, at, mine(cot, at) + scale * (weighted - scaled * mean))
 
-    gain_step(7)
-    gain_out[...] = gain_s[7, pl.ds(here["dp"], 1), :]
 
     for p in range(2):
-        total = outer(p, z)
         d_copy(1, 1 - p).wait()
         d_copy(2, p).wait()
-        out_share[p * PIECE : (p + 1) * PIECE, :] = (
-            total + side_r[1 - p].astype(F32) + near_r[p].astype(F32)
-        )
+        out_share[p * PIECE : (p + 1) * PIECE, :] += side_r[1 - p].astype(F32) + near_r[p].astype(F32)
     for p in range(3):
-        total = joint(p, xh)
         joint_pair(p).wait()
-        total = (total + pair_r[p].astype(F32)).T
+        total = (joint_own[p] + pair_r[p].astype(F32)).T
         if p < 2:
             query_share[:, p * PIECE : (p + 1) * PIECE] = total
         else:
             key_share[...] = total[:, :KC]
             value_share[...] = total[:, KC:]
+    gain_s[3] = gain_sum(2, gain_c, here["chip"], gain_s[2])
+    gain_out[...] = gain_s[3, pl.ds(here["dp"], 1), :]
+    for number in range(7):
+        gain_over(number).wait_send()
+        gain_chips(number).wait_send()
     for number in range(9):
         slice_copy(number).wait_send()
     for number in range(7):
@@ -613,7 +642,7 @@
         layer_kernel,
         out_shape=(
             shape(own_shape, BF), shape(own_shape, BF), shape((SLICE, QC), F32), shape((SLICE, KC), F32),
-            shape((SLICE, KC), F32), shape((QC, SLICE), F32), shape((1, SLICE), F32),
+            shape((SLICE, KC), F32), shape((QC, SLICE), F32), shape((1, 128), F32),
         ),
         in_specs=[at_vmem] * 3 + [at_any] * 4 + [at_vmem] * 3,
         out_specs=tuple([at_vmem] * 7),
@@ -625,14 +654,14 @@
             vmem((2, 2, TOK, SLICE), BF), vmem((2, 2, TOK, QC), BF), vmem((4, 2, TOK, QC + 2 * KC), BF),
             vmem((2, 2) + chunk, BF), vmem((2, 2) + chunk, BF), vmem((2, 2) + chunk, BF), vmem((2,) + chunk, BF),
             vmem((2,) + block, BF), vmem((2,) + block, BF), vmem((2,) + block, BF), vmem((3,) + block, BF),
-            vmem((8, 16, SLICE), F32), vmem((7, 16, SLICE), F32),
+            vmem((4, 16, 128), F32), vmem((8, 16, 128), F32), vmem((8, 16, 128), F32), vmem((4, 16, 128), F32),
             vmem((TOK, QC), F32), vmem((TOK, 2 * KC), F32),
             vmem((TOK, QC), BF), vmem((TOK, HD), BF), vmem((TOK, HD), BF),
             vmem((TOK, QC), BF),
-            vmem((HEADS, TOK, TOK), F32), vmem((ROWS, 128), F32), vmem(chunk, F32),
+            vmem((HEADS, TOK, TOK), F32), vmem((ROWS, 128), F32), vmem(chunk, F32), vmem((3,) + block, F32),
             dma((3,)), dma((32,)), dma((2, 8)), dma((2, SLOTS)), dma((2, 2)), dma((9,)), dma((4, 2)), dma((2,)), dma((2,)),
             dma((3,)), dma((2, 2)), dma((3,)), dma((2, 2)), dma((7,)), dma((4, 2)),
-            dma((3, 2)), dma((3, 2)), dma((3,)), dma((3,)), dma((4, 2, 2)), dma((4, 2, 2)), dma((7,)), dma((7,)),
+            dma((3, 2)), dma((3, 2)), dma((3,)), dma((3,)), dma((4, 2, 2)), dma((4, 2, 2)), dma((3, 7)), dma((3, 8)),
         ],
         compiler_params=pltpu.CompilerParams(
             collective_id=0, has_side_effects=True, vmem_limit_bytes=62 * MIB
@@ -642,7 +671,7 @@
         w_query, w_key, w_value, w_out, jnp.asarray(cosine), jnp.asarray(sine), jnp.asarray(bias),
     )
     share = D // 128
-    gain_share = lax.dynamic_slice_in_dim(gain_total.reshape(SLICE), lax.axis_index("tensor") * share, share, 0)
+    gain_share = lax.dynamic_slice_in_dim(gain_total.reshape(128), lax.rem(lax.axis_index("tensor"), 2) * share, share, 0)
     return (as_given(layer_out), as_given(input_grad)) + results(
         (query_share, key_share, value_share, out_share)
     ) + (gain_share,)

time: 163 us -> 151 us (0.926)
  the two profiles are of different devices: /device:TPU:1 before, /device:TPU:4 now
where the time goes in v3:
time: 151 us
  Pallas kernels  141 us (93%)
  local copies, waits for them, and re-layouts  9.04 us (6%)
    pallas_call x1, Pallas kernels, shards(): pl.pallas_call(layer_kernel, out_shape=(shape(own_shape, BF), shape(own_s...  138 us
    reshape x2, local copies, waits for them, and re-layouts, as_given(): return array.reshape(SEQ_ROWS, 2, D).transpose(1, 0, 2)  3.99 us
    reshape x2, local copies, waits for them, and re-layouts, rows_of(): return array.transpose(1, 0, 2).reshape(ROWS, D)  3.78 us
    pallas_call x1, Pallas kernels, results(): pl.pallas_call(copy_kernel, out_shape=tuple((jax.ShapeDtypeStruct(a.shape...  3.21 us

profile of v3, /device:TPU:4, one launch (start us, length us, event | category | flops | bytes accessed | tf_op | source)
XLA Modules:
  0.0 150.7 jit_solution(6572894769579616751)
XLA Ops:
  0.6 1.9 %reshape.31.hidden = bf16[24,8192]{1,0:T(8,128)(2,1)} reshape(bf16[12,2,8192]{2,1,0:T(2,128)(2,1)} %bitcast.7) | data formatting | bytes 786432 | tf_op jit(solution)/shard_map/reshape | solution.py:636
  2.5 1.9 %reshape.32.cot = bf16[24,8192]{1,0:T(8,128)(2,1)} reshape(bf16[12,2,8192]{2,1,0:T(2,128)(2,1)} %bitcast.8) | data formatting | bytes 786432 | tf_op jit(solution)/shard_map/reshape | solution.py:636
  4.4 137.8 %shard_map.153 = (bf16[24,8192]{1,0:T(8,128)(2,1)}, bf16[24,8192]{1,0:T(8,128)(2,1)}, f32[512,512]{1,0:T(8,128)}, f32[512,128]{1,0:T(8,128)}, f32[512,128]{1,0:T...) custom-call(bf16[24,8192]{1,0:T(8,128)(2,1)} %reshape.31.hidden, bf16[24,8192]{1,0:T(8,128)(2,1)} %reshape.32.cot, ...), custom_call_target="tpu_custom_call" | custom-call | tf_op jit(solution)/shard_map/pallas_call | solution.py:641
  142.3 1.3 dynamic-slice_bitcast_fusion
  143.5 2.0 %reshape.34 = bf16[12,2,8192]{2,1,0:T(2,128)(2,1)} reshape(bf16[24,8192]{1,0:T(8,128)(2,1)} %get-tuple-element.18) | data formatting | bytes 786432 | tf_op jit(solution)/shard_map/reshape | solution.py:639
  145.5 2.0 %reshape.35 = bf16[12,2,8192]{2,1,0:T(2,128)(2,1)} reshape(bf16[24,8192]{1,0:T(8,128)(2,1)} %get-tuple-element.19) | data formatting | bytes 786432 | tf_op jit(solution)/shard_map/reshape | solution.py:639
  147.5 3.2 %shard_map.154 = (f32[512,512]{1,0:T(8,128)}, f32[512,128]{1,0:T(8,128)}, f32[512,128]{1,0:T(8,128)}, f32[512,512]{1,0:T(8,128)}) custom-call(f32[512,512]{1,0:T(8,128)} %get-tuple-element.20.refs_0_, f32[512,128]{1,0:T(8,128)} %get-tuple-element.21.refs_1_, f32[512,128]{1,0:T(8,128)} %get-tuple-element.22.refs_2_, f32[512,512]{1,0:T(8,128)} %get-tuple-element.23.refs_3_), custom_call_target="tpu_custom_call" | custom-call | tf_op jit(solution)/shard_map/pallas_call | solution.py:605

commit v4 on v3

--- a/solution.py
+++ b/solution.py
@@ -76,12 +76,13 @@
 
 def layer_kernel(
     hidden, cot, gain, w_query, w_key, w_value, w_out, cosine, sine, bias,
-    layer_out, input_grad, query_share, key_share, value_share, out_share, gain_out,
-    wq, wkv, wo, rows_n, rows_c, flat_n, flat_c, got_n, got_c, passed, mixed, grads,
+    layer_hbm, input_grad, query_hbm, key_hbm, value_hbm, out_hbm, gain_out,
+    layer_out, query_share, key_share, value_share, out_share,
+    wq, wkv, wo, rows_n, rows_c, rows_g, flat_n, raw_c, got_n, got_c, passed, mixed, grads,
     t_far_r, t_side_r, t_near_r, t_pair_r, far_r, side_r, near_r, pair_r,
     gain_own, gain_t, gain_c, gain_s, query_acc, kv_acc, query_rot, key_rot, values, grad_mixed, probs,
-    inverse, summed, joint_own,
-    w_sems, wo_sems, a_send, a_recv, f_recv, s_send, s_recv, p_recv, own_sems, c_send, c_recv, h_send, h_recv, m_send, m_recv,
+    inverse,
+    out_sems, w_sems, wo_sems, a_send, a_recv, f_recv, s_send, s_recv, p_recv, own_sems, c_send, c_recv, h_send, h_recv, m_send, m_recv,
     d_send, d_recv, j_send, j_recv, t_send, t_recv, g_send, g_recv,
 ):
     here = place()
@@ -91,7 +92,7 @@
     own, mate = here["tensor"], y * 2 + 1 - xl
     toward = ((here["y_up"], y_up), (here["y_down"], y_down))
     toward_z = ((here["z_up"], z_up), (here["z_down"], z_down))
-    rows = (rows_n, rows_c)
+    rows, sums = (rows_n, rows_c), (rows_n, rows_g)
 
     loads = (
         pltpu.make_async_copy(w_query, wq, w_sems.at[0]),
@@ -110,11 +111,24 @@
     def _(b):
         load_out(b).start()
 
+    def leaving(number):
+        src, dst = (
+            (out_share, out_hbm), (layer_out, layer_hbm), (query_share, query_hbm), (key_share, key_hbm),
+            (value_share, value_hbm),
+        )[number]
+        return pltpu.make_async_copy(src, dst, out_sems.at[number])
+
+    def leave(number):
+        leaving(number).start()
+
     def mine(ref, at):
-        return ref[:, at].astype(F32)
+        return ref[:, :, at].astype(F32).reshape(ROWS, SLICE)
 
     def give(ref, at, block):
-        ref[:, at] = block.astype(BF)
+        ref[:, :, at] = block.reshape(SEQ_ROWS, 2, SLICE).astype(BF)
+
+    def cot_block(i, zh):
+        return 2 * ((i // 4) * 4 + 2 * zh + lax.rem(i, 2)) + lax.rem(i // 2, 2)
 
     def square(i, total):
         block = mine(hidden, cols(i))
@@ -131,7 +145,7 @@
         ]
         rows_n[own, :, cols(k)] = jnp.concatenate(normed, axis=0).astype(BF)
         rows_c[own, :, cols(k)] = jnp.concatenate(
-            [mine(cot, cols(2 * k + p)) for p in range(2)], axis=0
+            [mine(cot, cols(cot_block(k, zh))) for zh in range(2)], axis=0
         ).astype(BF)
 
     greet(
@@ -172,8 +186,10 @@
         if a:
             landed(a, y_down * 2)
             push(a, 5, y_down * 2, here["y_up"])
+            share(y_down * 2)
             landed(a, y_up * 2 + 1)
             push(a, 6, y_up * 2 + 1, here["y_down"])
+            share(y_up * 2 + 1)
             return
         for way in range(2):
             landed(a, (y_down, y_up)[way] * 2 + xl)
@@ -189,14 +205,20 @@
         push(a, 7, slot, here["x_lo"])
 
     def rest(a):
-        landed(a, y_down * 2 + (1 if a else 1 - xl))
-        landed(a, y_up * 2 + (0 if a else 1 - xl))
+        if a:
+            for slot in (y_down * 2 + 1, y_up * 2, y_far * 2, y_far * 2 + 1):
+                landed(a, slot)
+                share(slot)
+            return
+        landed(a, y_down * 2 + 1 - xl)
+        landed(a, y_up * 2 + 1 - xl)
         landed(a, y_far * 2 + 1 - xl)
-        if a:
-            landed(a, y_far * 2 + xl)
 
     def flatten(a, k):
         chunks = [rows[a][slot, :, cols(k)].astype(F32) for slot in range(SLOTS)]
+        return whole(chunks)
+
+    def whole(chunks):
         return [
             jnp.concatenate([c[p * ROWS : (p + 1) * ROWS] for c in chunks], axis=0).astype(BF) for p in range(2)
         ]
@@ -231,16 +253,18 @@
             ref = got_n.at[zs, cs]
             remote(ref, ref, s_send.at[0], s_recv.at[zs, cs], here["sibling"]).wait_recv()
 
-    def cot_copy(number):
-        cross = 1 - core
-        src, device = (
-            (flat_c.at[core, 1 - xh], "x_hi"), (flat_c.at[cross, 1 - xh], "x_hi_cross"),
-            (flat_c.at[cross, xh], "sibling"),
+    def cot_copy(number, slot):
+        side, parity, device = (
+            (xh, 1 - core, "sibling"), (1 - xh, core, "x_hi"), (1 - xh, 1 - core, "x_hi_cross"),
         )[number]
-        return remote(src, got_c.at[xh, core], c_send.at[number], c_recv.at[xh, core], here[device])
-
-    def own_cot():
-        return pltpu.make_async_copy(flat_c.at[core, xh], got_c.at[xh, core], own_sems.at[1])
+        src = rows_c.at[slot, :, cols(side * 2 + parity, 2 * SLICE)]
+        return remote(
+            src, raw_c.at[number, slot], c_send.at[slot, number], c_recv.at[number, slot], here[device]
+        )
+
+    def share(slot):
+        for number in (1, 2, 0):
+            cot_copy(number, slot).start()
 
     def mix_copy(number):
         device = ("x_hi", "x_hi_cross", "sibling")[number]
@@ -248,12 +272,16 @@
         return remote(ref, ref, h_send.at[number], h_recv.at[xh, core], here[device])
 
     def cross_wait():
-        own_cot().wait()
-        for xs, cs in ((xh, 1 - core), (1 - xh, core), (1 - xh, 1 - core)):
-            ref = got_c.at[xs, cs]
-            remote(ref, ref, c_send.at[0], c_recv.at[xs, cs], here["sibling"]).wait_recv()
+        for number, (xs, cs) in enumerate(((xh, 1 - core), (1 - xh, core), (1 - xh, 1 - core))):
             ref = mixed.at[xs, cs]
             remote(ref, ref, h_send.at[0], h_recv.at[xs, cs], here["sibling"]).wait_recv()
+            for slot in range(SLOTS):
+                ref = raw_c.at[number, slot]
+                remote(ref, ref, c_send.at[slot, 0], c_recv.at[number, slot], here["sibling"]).wait_recv()
+            for zl in range(2):
+                chunks = [raw_c[number, slot, :, zl * SLICE : (zl + 1) * SLICE].astype(F32) for slot in range(SLOTS)]
+                for zh, block in enumerate(whole(chunks)):
+                    got_c[xs, cs, 2 * zh + zl] = block
 
     def columns_copy(number):
         at, device = (
@@ -294,6 +322,8 @@
     push_along(1)
     push_mate(1)
     rest(0)
+    share(own)
+    share(mate)
 
     query_acc[...] = jnp.zeros_like(query_acc)
     kv_acc[...] = jnp.zeros_like(kv_acc)
@@ -344,7 +374,7 @@
 
     def to_chunks(a, k, blocks):
         for slot in range(SLOTS):
-            rows[a][slot, :, cols(k)] = jnp.concatenate(
+            sums[a][slot, :, cols(k)] = jnp.concatenate(
                 [b[slot * ROWS : (slot + 1) * ROWS] for b in blocks], axis=0
             ).astype(BF)
 
@@ -358,7 +388,7 @@
         device, at = toward[way]
         slot = (y_far * 2 + way, at * 2 + 1 - way, at * 2 + way)[kind]
         dst = (t_far_r, t_side_r, t_near_r)[kind].at[a, way]
-        return remote(rows[a].at[slot], dst, t_send.at[kind, a, way], t_recv.at[kind, a, way], device)
+        return remote(sums[a].at[slot], dst, t_send.at[kind, a, way], t_recv.at[kind, a, way], device)
 
     def t_start(a):
         for kind in range(2):
@@ -372,21 +402,21 @@
 
             @pl.loop(0, 8)
             def _(k, way=way, slot=slot):
-                rows[a][slot, :, cols(k)] = (
-                    rows[a][slot, :, cols(k)].astype(F32) + t_far_r[a, way, :, cols(k)].astype(F32)
+                sums[a][slot, :, cols(k)] = (
+                    sums[a][slot, :, cols(k)].astype(F32) + t_far_r[a, way, :, cols(k)].astype(F32)
                 ).astype(BF)
 
             t_copy(2, a, way).start()
 
     def t_total(a, side, k):
         return (
-            rows[a][y * 2 + side, :, cols(k)].astype(F32)
+            sums[a][y * 2 + side, :, cols(k)].astype(F32)
             + t_side_r[a, 1 - side, :, cols(k)].astype(F32)
             + t_near_r[a, side, :, cols(k)].astype(F32)
         )
 
     def t_pair(a):
-        return remote(rows[a].at[mate], t_pair_r.at[a], t_send.at[3, a, 0], t_recv.at[3, a, 0], here["x_lo"])
+        return remote(sums[a].at[mate], t_pair_r.at[a], t_send.at[3, a, 0], t_recv.at[3, a, 0], here["x_lo"])
 
     def t_settle(a):
         for way in range(2):
@@ -395,7 +425,7 @@
 
         @pl.loop(0, 8)
         def _(k):
-            rows[a][mate, :, cols(k)] = t_total(a, 1 - xl, k).astype(BF)
+            sums[a][mate, :, cols(k)] = t_total(a, 1 - xl, k).astype(BF)
 
         t_pair(a).start()
 
@@ -406,18 +436,16 @@
 
     query_acc[...] = jnp.zeros_like(query_acc)
 
-    for step, side in enumerate((1 - xh, xh)):
-        @pl.loop(0, 4)
-        def _(at, side=side):
-            k = side * 4 + at
-            for p, block in enumerate(flatten(1, k)):
-                flat_c[p, side, at] = block
-                for half in range(2):
-                    query_acc[:, half * PIECE : (half + 1) * PIECE] += dot(block, wo[half * 16 + 2 * k + p], 1, 1)
-
-        for number in ((0, 1), (2,))[step]:
-            cot_copy(number).start()
-    own_cot().start()
+    @pl.loop(0, 8)
+    def _(i):
+        for zh, block in enumerate(flatten(1, i)):
+            at = cot_block(i, zh)
+            for half in range(2):
+                query_acc[:, half * PIECE : (half + 1) * PIECE] += dot(block, wo[half * 16 + at], 1, 1)
+
+    for zl in range(2):
+        for zh, block in enumerate(flatten(1, (xh * 2 + core) * 2 + zl)):
+            got_c[xh, core, 2 * zh + zl] = block
     grad_mixed[...] = query_acc[...].astype(BF)
 
     def joint(p, side):
@@ -457,8 +485,6 @@
     columns_start()
     t_relay(0)
 
-    for copy in pushed[1]:
-        copy.wait_send()
 
     @pl.loop(0, 8)
     def _(k):
@@ -502,7 +528,14 @@
     for number in range(7):
         gain_over(number).start()
     t_start(1)
+    cross_wait()
     columns_pass()
+    for way in range(2):
+        wo[3 + way] = outer(way, z_far).astype(BF)
+        d_copy(0, way).start()
+    for way in range(2):
+        wo[5 + way] = outer(1 - way, toward_z[way][1]).astype(BF)
+        d_copy(1, way).start()
     t_settle(0)
     columns_last()
     t_relay(1)
@@ -511,29 +544,32 @@
     for p in range(3):
         wo[p] = joint(p, 1 - xh).astype(BF)
         joint_pair(p).start()
+    for way in range(2):
+        block = outer(way, toward_z[way][1])
+        d_copy(0, way).wait()
+        wo[7 + way] = (block + far_r[way].astype(F32)).astype(BF)
+        d_copy(2, way).start()
     gain_s[0] = gain_sum(0, gain_t, own, gain_own[y])
     gain_sibling().start()
-    cross_wait()
-    for way in range(2):
-        wo[3 + way] = outer(way, z_far).astype(BF)
-        d_copy(0, way).start()
-    for way in range(2):
-        wo[5 + way] = outer(1 - way, toward_z[way][1]).astype(BF)
-        d_copy(1, way).start()
     gain_sibling().wait()
     gain_s[2] = gain_s[0] + gain_s[1]
     for number in range(7):
         gain_chips(number).start()
     t_settle(1)
-    for way in range(2):
-        block = outer(way, toward_z[way][1])
-        d_copy(0, way).wait()
-        wo[7 + way] = (block + far_r[way].astype(F32)).astype(BF)
-        d_copy(2, way).start()
     for p in range(3):
-        joint_own[p] = joint(p, xh)
+        total = joint(p, xh).T
+        if p < 2:
+            query_share[:, p * PIECE : (p + 1) * PIECE] = total
+        else:
+            key_share[...] = total[:, :KC]
+            value_share[...] = total[:, KC:]
     for p in range(2):
         out_share[p * PIECE : (p + 1) * PIECE, :] = outer(p, z)
+    for p in range(2):
+        d_copy(1, 1 - p).wait()
+        d_copy(2, p).wait()
+        out_share[p * PIECE : (p + 1) * PIECE, :] += side_r[1 - p].astype(F32) + near_r[p].astype(F32)
+    leave(0)
     t_pair(0).wait()
 
     @pl.loop(0, 8)
@@ -543,12 +579,22 @@
             at = cols(2 * k + p)
             give(layer_out, at, mine(hidden, at) + total[p * ROWS : (p + 1) * ROWS])
 
+    leave(1)
+    for p in range(3):
+        joint_pair(p).wait()
+        total = pair_r[p].astype(F32).T
+        if p < 2:
+            query_share[:, p * PIECE : (p + 1) * PIECE] += total
+        else:
+            key_share[...] += total[:, :KC]
+            value_share[...] += total[:, KC:]
+    for number in range(2, 5):
+        leave(number)
     t_pair(1).wait()
     scale = inverse[:, :1]
 
     def weigh(k, total):
         block = t_total(1, xl, k) + t_pair_r[1, :, cols(k)].astype(F32)
-        summed[:, cols(k)] = block
         for p in range(2):
             at = cols(2 * k + p)
             scaled = mine(hidden, at) * scale
@@ -560,28 +606,22 @@
 
     @pl.loop(0, 8)
     def _(k):
-        block = summed[:, cols(k)]
+        block = t_total(1, xl, k) + t_pair_r[1, :, cols(k)].astype(F32)
         for p in range(2):
             at = cols(2 * k + p)
             scaled = mine(hidden, at) * scale
             weighted = block[p * ROWS : (p + 1) * ROWS] * gain[:, at]
             give(input_grad, at, mine(cot, at) + scale * (weighted - scaled * mean))
 
-
-    for p in range(2):
-        d_copy(1, 1 - p).wait()
-        d_copy(2, p).wait()
-        out_share[p * PIECE : (p + 1) * PIECE, :] += side_r[1 - p].astype(F32) + near_r[p].astype(F32)
-    for p in range(3):
-        joint_pair(p).wait()
-        total = (joint_own[p] + pair_r[p].astype(F32)).T
-        if p < 2:
-            query_share[:, p * PIECE : (p + 1) * PIECE] = total
-        else:
-            key_share[...] = total[:, :KC]
-            value_share[...] = total[:, KC:]
     gain_s[3] = gain_sum(2, gain_c, here["chip"], gain_s[2])
     gain_out[...] = gain_s[3, pl.ds(here["dp"], 1), :]
+    for copy in pushed[1]:
+        copy.wait_send()
+    for slot in range(SLOTS):
+        for number in range(3):
+            cot_copy(number, slot).wait_send()
+    for number in range(5):
+        leaving(number).wait()
     for number in range(7):
         gain_over(number).wait_send()
         gain_chips(number).wait_send()
@@ -590,7 +630,6 @@
     for number in range(7):
         columns_copy(number).wait_send()
     for number in range(3):
-        cot_copy(number).wait_send()
         mix_copy(number).wait_send()
 
 
@@ -630,13 +669,13 @@
     at_any = pl.BlockSpec(memory_space=pl.ANY)
     shape = jax.ShapeDtypeStruct
     cosine, sine, bias = tables(SEQ_ROWS)
-    own_shape = (ROWS, D)
+    own_shape = (SEQ_ROWS, 2, D)
 
     def rows_of(array):
-        return array.transpose(1, 0, 2).reshape(ROWS, D)
+        return array.transpose(1, 0, 2)
 
     def as_given(array):
-        return array.reshape(SEQ_ROWS, 2, D).transpose(1, 0, 2)
+        return array.transpose(1, 0, 2)
 
     layer_out, input_grad, query_share, key_share, value_share, out_share, gain_total = pl.pallas_call(
         layer_kernel,
@@ -645,11 +684,13 @@
             shape((SLICE, KC), F32), shape((QC, SLICE), F32), shape((1, 128), F32),
         ),
         in_specs=[at_vmem] * 3 + [at_any] * 4 + [at_vmem] * 3,
-        out_specs=tuple([at_vmem] * 7),
+        out_specs=(at_any, at_vmem, at_any, at_any, at_any, at_any, at_vmem),
         scratch_shapes=[
+            vmem((SEQ_ROWS, 2, D), BF), vmem((SLICE, QC), F32), vmem((SLICE, KC), F32), vmem((SLICE, KC), F32),
+            vmem((QC, SLICE), F32),
             vmem((D, QC), BF), vmem((D, 2 * KC), BF), vmem((32,) + block, BF),
-            vmem((SLOTS,) + chunk, BF), vmem((SLOTS,) + chunk, BF),
-            vmem((2, 4, 2, TOK, SLICE), BF), vmem((2, 2, 4, TOK, SLICE), BF),
+            vmem((SLOTS,) + chunk, BF), vmem((SLOTS,) + chunk, BF), vmem((SLOTS,) + chunk, BF),
+            vmem((2, 4, 2, TOK, SLICE), BF), vmem((3, SLOTS, PAIR, 2 * SLICE), BF),
             vmem((4, 2, 2, TOK, SLICE), BF), vmem((2, 2, 4, TOK, SLICE), BF),
             vmem((2, 2, TOK, SLICE), BF), vmem((2, 2, TOK, QC), BF), vmem((4, 2, TOK, QC + 2 * KC), BF),
             vmem((2, 2) + chunk, BF), vmem((2, 2) + chunk, BF), vmem((2, 2) + chunk, BF), vmem((2,) + chunk, BF),
@@ -658,9 +699,9 @@
             vmem((TOK, QC), F32), vmem((TOK, 2 * KC), F32),
             vmem((TOK, QC), BF), vmem((TOK, HD), BF), vmem((TOK, HD), BF),
             vmem((TOK, QC), BF),
-            vmem((HEADS, TOK, TOK), F32), vmem((ROWS, 128), F32), vmem(chunk, F32), vmem((3,) + block, F32),
-            dma((3,)), dma((32,)), dma((2, 8)), dma((2, SLOTS)), dma((2, 2)), dma((9,)), dma((4, 2)), dma((2,)), dma((2,)),
-            dma((3,)), dma((2, 2)), dma((3,)), dma((2, 2)), dma((7,)), dma((4, 2)),
+            vmem((HEADS, TOK, TOK), F32), vmem((ROWS, 128), F32),
+            dma((5,)), dma((3,)), dma((32,)), dma((2, 8)), dma((2, SLOTS)), dma((2, 2)), dma((9,)), dma((4, 2)), dma((2,)), dma((2,)),
+            dma((SLOTS, 3)), dma((3, SLOTS)), dma((3,)), dma((2, 2)), dma((7,)), dma((4, 2)),
             dma((3, 2)), dma((3, 2)), dma((3,)), dma((3,)), dma((4, 2, 2)), dma((4, 2, 2)), dma((3, 7)), dma((3, 8)),
         ],
         compiler_params=pltpu.CompilerParams(
@@ -672,9 +713,10 @@
     )
     share = D // 128
     gain_share = lax.dynamic_slice_in_dim(gain_total.reshape(128), lax.rem(lax.axis_index("tensor"), 2) * share, share, 0)
-    return (as_given(layer_out), as_given(input_grad)) + results(
-        (query_share, key_share, value_share, out_share)
-    ) + (gain_share,)
+    layer_out, input_grad, *weight_shares = results(
+        (layer_out, input_grad, query_share, key_share, value_share, out_share)
+    )
+    return (as_given(layer_out), as_given(input_grad), *weight_shares, gain_share)
 
 
 def solution(mesh):

time: 151 us -> 138 us (0.914)
  the two profiles are of different devices: /device:TPU:4 before, /device:TPU:1 now
where the time goes in v4:
time: 138 us; the launch traced here: 137 us
  Pallas kernels  135 us (98%)
    pallas_call x1, Pallas kernels, shards(): pl.pallas_call(layer_kernel, out_shape=(shape(own_shape, BF), shape(own_s...  131 us
    pallas_call x1, Pallas kernels, results(): pl.pallas_call(copy_kernel, out_shape=tuple((jax.ShapeDtypeStruct(a.shape...  3.72 us

profile of v4, /device:TPU:1, one launch (start us, length us, event | category | flops | bytes accessed | tf_op | source)
XLA Modules:
  0.0 136.9 jit_solution(1039794641150025916)
XLA Ops:
  0.6 131.2 %shard_map.153 = (bf16[12,2,8192]{2,1,0:T(2,128)(2,1)}, bf16[12,2,8192]{2,1,0:T(2,128)(2,1)}, f32[512,512]{1,0:T(8,128)}, f32[512,128]{1,0:T(8,128)}, f32[512,12...) custom-call(bf16[12,2,8192]{2,1,0:T(2,128)(2,1)} %bitcast.7, bf16[12,2,8192]{2,1,0:T(2,128)(2,1)} %bitcast.8, ...), custom_call_target="tpu_custom_call" | custom-call | tf_op jit(solution)/shard_map/pallas_call | solution.py:680
  131.9 1.3 dynamic-slice_bitcast_fusion
  133.2 3.7 %shard_map.154 = (bf16[12,2,8192]{2,1,0:T(2,128)(2,1)}, bf16[12,2,8192]{2,1,0:T(2,128)(2,1)}, f32[512,512]{1,0:T(8,128)}, f32[512,128]{1,0:T(8,128)}, f32[512,128]{1,0:T(8,128)}, /*index=5*/f32[512,512]{1,0:T(8,128)}) custom-call(bf16[12,2,8192]{2,1,0:T(2,128)(2,1)} %get-tuple-element.20.refs_0_, bf16[12,2,8192]{2,1,0:T(2,128)(2,1)} %get-tuple-element.21.refs_1_, ...), custom_call_target="tpu_custom_call" | custom-call | tf_op jit(solution)/shard_map/pallas_call | solution.py:644
